TPU v7x, 128 devices: a whole 4x4x4 slice. The times are simulated.
128 devices in a mesh: pipe: 8 (over z, core), dp: 8 (over x_lo, y), tensor: 2 (over x_hi).
Axes of the slice: x: 4 (x_hi: 2, x_lo: 2; x = x_hi * 2 + x_lo), y: 4, z: 4, core: 2. Of those that a mesh axis runs over, the one named last changes fastest.
Arguments:
- tokens: bfloat16 [4, 64, 4096], replicated, may hold values from -6 to 6
- slice_order: int32 [4], replicated, may hold values from 0 to 3, each once
- norm_gain: float32 [8, 4096], P('pipe'), may hold values from 0.5 to 1.5
- w_z: bfloat16 [8, 4096, 8192], P('pipe', None, ('dp', 'tensor')), may hold values from -0.09375 to 0.09375
- w_x: bfloat16 [8, 4096, 8192], P('pipe', None, ('dp', 'tensor')), may hold values from -0.09375 to 0.09375
- w_bc: bfloat16 [8, 4096, 2048], P('pipe', None, 'dp'), may hold values from -0.09375 to 0.09375
- w_dt: bfloat16 [8, 4096, 128], P('pipe', None, ('dp', 'tensor')), may hold values from -0.09375 to 0.09375
- conv_x: float32 [8, 4, 8192], P('pipe', None, ('dp', 'tensor')), may hold values from -3 to 3
- conv_bc: float32 [8, 4, 2048], P('pipe', None, 'dp'), may hold values from -3 to 3
- dt_bias: float32 [8, 128], P('pipe', ('dp', 'tensor')), may hold values from -3 to 0
- decay_rate: float32 [8, 128], P('pipe', ('dp', 'tensor')), may hold values from 0.005 to 0.5
- skip_gain: float32 [8, 128], P('pipe', ('dp', 'tensor')), may hold values from 0.5 to 1.5
- inner_gain: float32 [8, 8192], P('pipe', ('dp', 'tensor')), may hold values from 0.5 to 1.5
- w_out: bfloat16 [8, 8192, 4096], P('pipe', ('dp', 'tensor')), may hold values from -0.0625 to 0.0625
Outputs:
- activations: bfloat16 [8, 4, 64, 4096], P('pipe', None, ('dp', 'tensor'))
Inputs may be any that keep to these rules, and one draw needn't show every extreme that they name: slice_order is a permutation of the slices.
All inputs are finite; a program needn't handle non-finite values.
Results may differ from a plain program's by a relative error of at most 0.029.
Values may be sent and summed in bfloat16 or wider, within the bound.
A program may use at most 64 MiB of HBM per device.

v0:
```python
import jax
import jax.numpy as jnp
from jax import lax
from jax.sharding import PartitionSpec as P

HEADS = 128
STATE = 128
GROUPS = 8
CONV = 4


EPS = 1e-05
HIGH = lax.Precision.HIGHEST


def shifted(value, axis, steps):
    count = lax.axis_size(axis)
    leading, last = (max(0, -steps), min(count, count - steps))
    return lax.ppermute(value, axis, [(source, source + steps) for source in range(leading, last)])


def mixer_part(
    rows_in,
    conv_state,
    bc_state,
    ssm_state,
    norm_gain,
    w_z,
    w_x,
    w_bc,
    w_dt,
    conv_x,
    conv_bc,
    dt_bias,
    decay_rate,
    skip_gain,
    head_pick,
    group_pick,
):
    length = rows_in.shape[0]
    heads = w_dt.shape[1]
    head_dim = w_x.shape[1] // heads
    taps = conv_x.shape[0]
    values = rows_in.astype(jnp.float32)
    normed = (
        values * lax.rsqrt(jnp.mean(values * values, axis=1, keepdims=True) + EPS) * norm_gain
    ).astype(jnp.bfloat16)
    gate_in = jnp.dot(normed, w_z, preferred_element_type=jnp.float32)
    x_raw = jnp.dot(normed, w_x, preferred_element_type=jnp.float32)
    bc_raw = jnp.dot(normed, w_bc, preferred_element_type=jnp.float32)
    dt_raw = jnp.dot(normed, w_dt, preferred_element_type=jnp.float32)
    x_full = jnp.concatenate([conv_state, x_raw], axis=0)
    bc_full = jnp.concatenate([bc_state, bc_raw], axis=0)
    x_conv = jnp.zeros_like(x_raw)
    bc_conv = jnp.zeros_like(bc_raw)
    for k in range(taps):
        x_conv = x_conv + conv_x[k] * x_full[k : k + length]
        bc_conv = bc_conv + conv_bc[k] * bc_full[k : k + length]
    x_act = jax.nn.silu(x_conv)
    bc_act = jax.nn.silu(bc_conv)
    groups_here = head_pick.shape[1]
    bc_groups = bc_act.reshape(length, groups_here, 2 * STATE)
    b_head = jnp.einsum("hg,tgn->thn", head_pick, bc_groups[:, :, :STATE], precision=HIGH)
    c_head = jnp.einsum("hg,tgn->thn", head_pick, bc_groups[:, :, STATE:], precision=HIGH)
    step_size = jax.nn.softplus(dt_raw + dt_bias)
    cumulated = jnp.cumsum(-step_size * decay_rate, axis=0)
    x_heads = x_act.reshape(length, heads, head_dim)
    scores = jnp.einsum("thn,shn->hts", c_head, b_head, precision=HIGH)
    differences = cumulated.T[:, :, None] - cumulated.T[:, None, :]
    below_diag = (jnp.arange(length)[:, None] >= jnp.arange(length)[None, :])[None, :, :]
    decays = jnp.where(below_diag, jnp.exp(jnp.where(below_diag, differences, 0.0)), 0.0)
    weighted = x_heads * step_size[:, :, None]
    outputs = jnp.einsum("hts,shp->thp", scores * decays, weighted, precision=HIGH)
    outputs = outputs + jnp.exp(cumulated)[:, :, None] * jnp.einsum(
        "thn,hpn->thp", c_head, ssm_state, precision=HIGH
    )
    outputs = outputs + skip_gain[None, :, None] * x_heads
    remaining = jnp.exp(cumulated[-1][None, :] - cumulated) * step_size
    new_state = jnp.exp(cumulated[-1])[:, None, None] * ssm_state + jnp.einsum(
        "sh,shp,shn->hpn", remaining, x_heads, b_head, precision=HIGH
    )
    gated = outputs.reshape(length, heads * head_dim) * jax.nn.silu(gate_in)
    squares = jnp.dot(gated * gated, group_pick, precision=HIGH)
    return (gated, squares, x_full[length:], bc_full[length:], new_state)


def local(
    tokens,
    slice_order,
    norm_gain,
    w_z,
    w_x,
    w_bc,
    w_dt,
    conv_x,
    conv_bc,
    dt_bias,
    decay_rate,
    skip_gain,
    inner_gain,
    w_out,
):
    sections = lax.axis_size("pipe")
    section = lax.axis_index("pipe")
    members = lax.axis_size(("dp", "tensor"))
    member = lax.axis_index(("dp", "tensor"))
    half_index = lax.axis_index("tensor")
    slices = slice_order.shape[0]
    length = tokens.shape[1]
    width = tokens.shape[2]
    share = length // members
    heads = w_dt.shape[2]
    inner = w_x.shape[2]
    head_dim = inner // heads
    groups_here = w_bc.shape[2] // (2 * STATE)
    heads_per_group = HEADS // GROUPS
    channels = heads_per_group * head_dim
    head_pick = (
        jnp.arange(groups_here)[None, :]
        == ((half_index * heads + jnp.arange(heads)) // heads_per_group)[:, None]
    ).astype(jnp.float32)
    group_pick = jnp.repeat(head_pick, head_dim, axis=0)
    gain_in = norm_gain[0]
    z_weight = w_z[0]
    x_weight = w_x[0]
    bc_weight = w_bc[0]
    dt_weight = w_dt[0]
    x_taps = conv_x[0]
    bc_taps = conv_bc[0]
    bias_dt = dt_bias[0]
    rates = decay_rate[0]
    skips = skip_gain[0]
    gain_inner = inner_gain[0]
    out_weight = w_out[0]
    ticks = slices + sections - 1

    def tick(t, carry):
        arriving, conv_state, bc_state, ssm_state, saved = carry
        position = t - section
        valid = (position >= 0) & (position < slices)
        place = jnp.clip(position, 0, slices - 1)
        source = slice_order[place]
        fresh = lax.dynamic_index_in_dim(tokens, source, 0, keepdims=False)
        current = jnp.where(section == 0, fresh, arriving)

        def active():
            return mixer_part(
                current,
                conv_state,
                bc_state,
                ssm_state,
                gain_in,
                z_weight,
                x_weight,
                bc_weight,
                dt_weight,
                x_taps,
                bc_taps,
                bias_dt,
                rates,
                skips,
                head_pick,
                group_pick,
            )

        def resting():
            return (
                jnp.zeros((length, inner), jnp.float32),
                jnp.zeros((length, groups_here), jnp.float32),
                conv_state,
                bc_state,
                ssm_state,
            )

        gated, squares, conv_next, bc_next, ssm_next = lax.cond(valid, active, resting)
        totals = lax.psum(squares, "tensor")
        scale = lax.rsqrt(jnp.dot(totals, group_pick.T, precision=HIGH) / channels + EPS)
        mixed = (gated * scale * gain_inner).astype(jnp.bfloat16)
        terms = lax.cond(
            valid,
            lambda: jnp.dot(mixed, out_weight, preferred_element_type=jnp.float32),
            lambda: jnp.zeros((length, width), jnp.float32),
        )
        summed = lax.psum(terms, ("dp", "tensor"))
        updated = (current.astype(jnp.float32) + summed).astype(jnp.bfloat16)
        kept = lax.dynamic_slice_in_dim(updated, member * share, share, 0)
        arriving_next = shifted(updated, "pipe", 1)
        previous = lax.dynamic_index_in_dim(saved, place, 0, keepdims=False)
        stored = jnp.where(valid, kept, previous)
        saved = lax.dynamic_update_index_in_dim(saved, stored, place, 0)
        return (arriving_next, conv_next, bc_next, ssm_next, saved)

    arriving_start = jnp.zeros((length, width), jnp.bfloat16)
    start_carry = (
        arriving_start,
        jnp.zeros((CONV - 1, inner), jnp.float32),
        jnp.zeros((CONV - 1, groups_here * 2 * STATE), jnp.float32),
        jnp.zeros((heads, head_dim, STATE), jnp.float32),
        jnp.zeros((slices, share, width), jnp.bfloat16),
    )
    final_carry = lax.fori_loop(0, ticks, tick, start_carry)
    return final_carry[4][None]


def solution(mesh):
    placed = (
        P(),
        P(),
        P("pipe", None),
        P("pipe", None, ("dp", "tensor")),
        P("pipe", None, ("dp", "tensor")),
        P("pipe", None, "dp"),
        P("pipe", None, ("dp", "tensor")),
        P("pipe", None, ("dp", "tensor")),
        P("pipe", None, "dp"),
        P("pipe", ("dp", "tensor")),
        P("pipe", ("dp", "tensor")),
        P("pipe", ("dp", "tensor")),
        P("pipe", ("dp", "tensor")),
        P("pipe", ("dp", "tensor"), None),
    )
    return jax.shard_map(
        local,
        mesh=mesh,
        in_specs=placed,
        out_specs=P("pipe", None, ("dp", "tensor"), None),
        check_vma=False,
    )
```

profile of v0, /device:TPU:99, one launch (start us, length us, event | category | flops | bytes accessed | tf_op | source)
XLA Modules:
  0.0 1418.9 jit_solution(8965363535394944863)
XLA Ops:
  6.7 1405.1 %while.25 = (s32[]{:T(128)}, bf16[64,4096]{1,0:T(8,128)(2,1)S(1)}, f32[3,512]{1,0:T(4,128)S(1)}, f32[3,256]{1,0:T(4,128)S(1)}, f32[8,64,128]{2,1,0:T(8,128)S(1)}...) while((s32[]{:T(128)}, bf16[64,4096]{1,0:T(8,128)(2,1)S(1)}, ...), condition=%wide.region_9.10_spmd.clone.clone, body=%wide.region_0.9_spmd.clone.clone.sunk | while | flops 1128424704 | bytes 39009428 | solution.py:201
  11.8 5.3 psum.32
  19.4 102.1 %all-reduce.2.cloned.1.call-done = f32[64,4096]{1,0:T(8,128)} async-done(((f32[64,4096]{1,0:T(8,128)}), f32[64,4096]{1,0:T(8,128)}) %all-reduce.2.cloned.1.call-update) | async-done | bytes 1048592 | tf_op jit(solution)/shard_map/while/body/eval_jaxpr/psum | solution.py:184
  133.4 5.3 psum.32
  141.0 105.7 %all-reduce.2.cloned.1.call-done = f32[64,4096]{1,0:T(8,128)} async-done(((f32[64,4096]{1,0:T(8,128)}), f32[64,4096]{1,0:T(8,128)}) %all-reduce.2.cloned.1.call-update) | async-done | bytes 1048592 | tf_op jit(solution)/shard_map/while/body/eval_jaxpr/psum | solution.py:184
  258.5 5.3 psum.32
  266.1 109.0 %all-reduce.2.cloned.1.call-done = f32[64,4096]{1,0:T(8,128)} async-done(((f32[64,4096]{1,0:T(8,128)}), f32[64,4096]{1,0:T(8,128)}) %all-reduce.2.cloned.1.call-update) | async-done | bytes 1048592 | tf_op jit(solution)/shard_map/while/body/eval_jaxpr/psum | solution.py:184
  386.9 5.3 psum.32
  394.5 109.0 %all-reduce.2.cloned.1.call-done = f32[64,4096]{1,0:T(8,128)} async-done(((f32[64,4096]{1,0:T(8,128)}), f32[64,4096]{1,0:T(8,128)}) %all-reduce.2.cloned.1.call-update) | async-done | bytes 1048592 | tf_op jit(solution)/shard_map/while/body/eval_jaxpr/psum | solution.py:184
  522.9 110.6 %all-reduce.2.cloned.1.call-done = f32[64,4096]{1,0:T(8,128)} async-done(((f32[64,4096]{1,0:T(8,128)}), f32[64,4096]{1,0:T(8,128)}) %all-reduce.2.cloned.1.call-update) | async-done | bytes 1048592 | tf_op jit(solution)/shard_map/while/body/eval_jaxpr/psum | solution.py:184
  653.0 110.6 %all-reduce.2.cloned.1.call-done = f32[64,4096]{1,0:T(8,128)} async-done(((f32[64,4096]{1,0:T(8,128)}), f32[64,4096]{1,0:T(8,128)}) %all-reduce.2.cloned.1.call-update) | async-done | bytes 1048592 | tf_op jit(solution)/shard_map/while/body/eval_jaxpr/psum | solution.py:184
  783.0 110.6 %all-reduce.2.cloned.1.call-done = f32[64,4096]{1,0:T(8,128)} async-done(((f32[64,4096]{1,0:T(8,128)}), f32[64,4096]{1,0:T(8,128)}) %all-reduce.2.cloned.1.call-update) | async-done | bytes 1048592 | tf_op jit(solution)/shard_map/while/body/eval_jaxpr/psum | solution.py:184
  904.7 15.9 %conditional.8 = (f32[64,512]{1,0:T(8,128)}, f32[64,1]{0,1:T(1,128)S(1)}, f32[3,512]{1,0:T(4,128)S(1)}, f32[3,256]{1,0:T(4,128)S(1)}, f32[8,64,128]{2,1,0:T(8,128)S(1)}) conditional(s32[]{:T(128)} %convert_element_type.111, (f32[3,512]{1,0:T(4,128)S(1)}, f32[3,256]{1,0:T(4,128)S(1)}, f32[8,64,128]{2,1,0:T(8,128)S(1)}) %tuple.76, (f32[4,512]{1,0:T(4,128)}, ...), branch_computations={%region_1.1_spmd, %region_2.4_spmd} | conditional | flops 858465344 | bytes 17067680 | solution.py:175
  920.7 5.3 psum.32
  931.2 92.4 %all-reduce.2.cloned.1.call-done = f32[64,4096]{1,0:T(8,128)} async-done(((f32[64,4096]{1,0:T(8,128)}), f32[64,4096]{1,0:T(8,128)}) %all-reduce.2.cloned.1.call-update) | async-done | bytes 1048592 | tf_op jit(solution)/shard_map/while/body/eval_jaxpr/psum | solution.py:184
  1034.8 15.9 %conditional.8 = (f32[64,512]{1,0:T(8,128)}, f32[64,1]{0,1:T(1,128)S(1)}, f32[3,512]{1,0:T(4,128)S(1)}, f32[3,256]{1,0:T(4,128)S(1)}, f32[8,64,128]{2,1,0:T(8,128)S(1)}) conditional(s32[]{:T(128)} %convert_element_type.111, (f32[3,512]{1,0:T(4,128)S(1)}, f32[3,256]{1,0:T(4,128)S(1)}, f32[8,64,128]{2,1,0:T(8,128)S(1)}) %tuple.76, (f32[4,512]{1,0:T(4,128)}, ...), branch_computations={%region_1.1_spmd, %region_2.4_spmd} | conditional | flops 858465344 | bytes 17067680 | solution.py:175
  1050.7 5.3 psum.32
  1061.3 92.2 %all-reduce.2.cloned.1.call-done = f32[64,4096]{1,0:T(8,128)} async-done(((f32[64,4096]{1,0:T(8,128)}), f32[64,4096]{1,0:T(8,128)}) %all-reduce.2.cloned.1.call-update) | async-done | bytes 1048592 | tf_op jit(solution)/shard_map/while/body/eval_jaxpr/psum | solution.py:184
  1164.6 15.9 %conditional.8 = (f32[64,512]{1,0:T(8,128)}, f32[64,1]{0,1:T(1,128)S(1)}, f32[3,512]{1,0:T(4,128)S(1)}, f32[3,256]{1,0:T(4,128)S(1)}, f32[8,64,128]{2,1,0:T(8,128)S(1)}) conditional(s32[]{:T(128)} %convert_element_type.111, (f32[3,512]{1,0:T(4,128)S(1)}, f32[3,256]{1,0:T(4,128)S(1)}, f32[8,64,128]{2,1,0:T(8,128)S(1)}) %tuple.76, (f32[4,512]{1,0:T(4,128)}, ...), branch_computations={%region_1.1_spmd, %region_2.4_spmd} | conditional | flops 858465344 | bytes 17067680 | solution.py:175
  1180.5 5.3 psum.32
  1191.1 92.2 %all-reduce.2.cloned.1.call-done = f32[64,4096]{1,0:T(8,128)} async-done(((f32[64,4096]{1,0:T(8,128)}), f32[64,4096]{1,0:T(8,128)}) %all-reduce.2.cloned.1.call-update) | async-done | bytes 1048592 | tf_op jit(solution)/shard_map/while/body/eval_jaxpr/psum | solution.py:184
  1294.5 15.9 %conditional.8 = (f32[64,512]{1,0:T(8,128)}, f32[64,1]{0,1:T(1,128)S(1)}, f32[3,512]{1,0:T(4,128)S(1)}, f32[3,256]{1,0:T(4,128)S(1)}, f32[8,64,128]{2,1,0:T(8,128)S(1)}) conditional(s32[]{:T(128)} %convert_element_type.111, (f32[3,512]{1,0:T(4,128)S(1)}, f32[3,256]{1,0:T(4,128)S(1)}, f32[8,64,128]{2,1,0:T(8,128)S(1)}) %tuple.76, (f32[4,512]{1,0:T(4,128)}, ...), branch_computations={%region_1.1_spmd, %region_2.4_spmd} | conditional | flops 858465344 | bytes 17067680 | solution.py:175
  1310.4 5.3 psum.32
  1321.0 84.0 %all-reduce.2.cloned.1.call-done = f32[64,4096]{1,0:T(8,128)} async-done(((f32[64,4096]{1,0:T(8,128)}), f32[64,4096]{1,0:T(8,128)}) %all-reduce.2.cloned.1.call-update) | async-done | bytes 1048592 | tf_op jit(solution)/shard_map/while/body/eval_jaxpr/psum | solution.py:184
  (393 shorter events, 239.5 us)
Async XLA Ops:
  6.7 114.8 %all-reduce.2.cloned.1.call-start = ((), (), s32[]{:S(2)}) async-start(), calls=%async_computation | async-start | bytes 2097152 | tf_op jit(solution)/shard_map/while/body/eval_jaxpr/psum | solution.py:184
  122.8 5.5 collective-permute-start
  128.3 118.3 %all-reduce.2.cloned.1.call-start = ((), (), s32[]{:S(2)}) async-start(), calls=%async_computation | async-start | bytes 2097152 | tf_op jit(solution)/shard_map/while/body/eval_jaxpr/psum | solution.py:184
  248.0 5.5 collective-permute-start
  253.5 121.6 %all-reduce.2.cloned.1.call-start = ((), (), s32[]{:S(2)}) async-start(), calls=%async_computation | async-start | bytes 2097152 | tf_op jit(solution)/shard_map/while/body/eval_jaxpr/psum | solution.py:184
  376.4 5.5 collective-permute-start
  381.9 121.6 %all-reduce.2.cloned.1.call-start = ((), (), s32[]{:S(2)}) async-start(), calls=%async_computation | async-start | bytes 2097152 | tf_op jit(solution)/shard_map/while/body/eval_jaxpr/psum | solution.py:184
  504.8 5.5 collective-permute-start
  510.3 123.2 %all-reduce.2.cloned.1.call-start = ((), (), s32[]{:S(2)}) async-start(), calls=%async_computation | async-start | bytes 2097152 | tf_op jit(solution)/shard_map/while/body/eval_jaxpr/psum | solution.py:184
  634.8 5.5 collective-permute-start
  640.3 123.2 %all-reduce.2.cloned.1.call-start = ((), (), s32[]{:S(2)}) async-start(), calls=%async_computation | async-start | bytes 2097152 | tf_op jit(solution)/shard_map/while/body/eval_jaxpr/psum | solution.py:184
  764.9 5.5 collective-permute-start
  770.4 123.2 %all-reduce.2.cloned.1.call-start = ((), (), s32[]{:S(2)}) async-start(), calls=%async_computation | async-start | bytes 2097152 | tf_op jit(solution)/shard_map/while/body/eval_jaxpr/psum | solution.py:184
  894.9 5.5 collective-permute-start
  900.4 123.2 %all-reduce.2.cloned.1.call-start = ((), (), s32[]{:S(2)}) async-start(), calls=%async_computation | async-start | bytes 2097152 | tf_op jit(solution)/shard_map/while/body/eval_jaxpr/psum | solution.py:184
  904.7 21.4 %copy-start.4 = (f32[1,512]{1,0:T(1,128)S(1)}, f32[1,512]{1,0:T(1,128)}, u32[]{:S(2)}) copy-start(f32[1,512]{1,0:T(1,128)} %get-tuple-element.1090) | copy-start | bytes 6148 | tf_op jit(solution)/shard_map/while
  1024.9 5.5 collective-permute-start
  1030.4 123.0 %all-reduce.2.cloned.1.call-start = ((), (), s32[]{:S(2)}) async-start(), calls=%async_computation | async-start | bytes 2097152 | tf_op jit(solution)/shard_map/while/body/eval_jaxpr/psum | solution.py:184
  1034.8 21.4 %copy-start.4 = (f32[1,512]{1,0:T(1,128)S(1)}, f32[1,512]{1,0:T(1,128)}, u32[]{:S(2)}) copy-start(f32[1,512]{1,0:T(1,128)} %get-tuple-element.1090) | copy-start | bytes 6148 | tf_op jit(solution)/shard_map/while
  1154.8 5.5 collective-permute-start
  1160.3 123.0 %all-reduce.2.cloned.1.call-start = ((), (), s32[]{:S(2)}) async-start(), calls=%async_computation | async-start | bytes 2097152 | tf_op jit(solution)/shard_map/while/body/eval_jaxpr/psum | solution.py:184
  1284.6 5.5 collective-permute-start
  1290.1 114.8 %all-reduce.2.cloned.1.call-start = ((), (), s32[]{:S(2)}) async-start(), calls=%async_computation | async-start | bytes 2097152 | tf_op jit(solution)/shard_map/while/body/eval_jaxpr/psum | solution.py:184
  1406.3 5.5 collective-permute-start
  (33 other events, 176.7 us)
Sparse Core Ops, SparseCore 0:
  19.5 101.9 all-reduce.1
  141.1 105.5 all-reduce.1
  266.2 108.8 all-reduce.1
  394.6 108.8 all-reduce.1
  523.0 110.4 all-reduce.1
  653.1 110.4 all-reduce.1
  783.1 110.4 all-reduce.1
  931.3 92.2 all-reduce.1
  1061.4 92.0 all-reduce.1
  1191.2 92.0 all-reduce.1
  1321.1 83.8 all-reduce.1
where the time goes:
time: 1430 us; the launch traced here: 1420 us
  waiting for transfers between devices  1160 us (81%)
  matrix products  66.3 us (5%)
  blocking collectives  58.1 us (4%)
  other arithmetic  40.6 us (3%)
  local copies, waits for them, and re-layouts  39 us (3%)
  loops' own time  23.5 us (2%)
  starting transfers between devices  14.3 us (1%)
    psum x11, waiting for transfers between devices, tick(): summed = lax.psum(terms, ('dp', 'tensor'))  1120 us
    psum x11, blocking collectives, tick(): totals = lax.psum(squares, 'tensor')  58.1 us
    ppermute x11, waiting for transfers between devices, shifted(): lax.ppermute(value, axis, [(source, source + steps) for source in range(l...  45.6 us
  transfers between devices with their start and end apart: 22, of which 22 were waited for; matrix products, arithmetic and copies ran while one was open for 0% of the time, Pallas kernels for 0%

commit v1 on v0

v1 whole, which is shorter than its diff:
```python
import functools

import jax
import jax.numpy as jnp
from jax import lax
from jax.experimental import pallas as pl
from jax.experimental.pallas import tpu as pltpu
from jax.sharding import PartitionSpec as P

MESH = pl.DeviceIdType.MESH
F32 = jnp.float32
BF16 = jnp.bfloat16
EPS = 1e-05
HIGH = lax.Precision.HIGHEST

SECTIONS = 8
MEMBERS = 16
SLICES = 4
LENGTH = 64
WIDTH = 4096
STATE = 128
CONV = 4
HEADS = 8
HEAD_DIM = 64
INNER = HEADS * HEAD_DIM
CHANNELS = 1024
ROWS = 16
COLS = 1024
WIDE = COLS + 128


def split_lanes(sums):
    high = sums.astype(BF16).astype(F32)
    lanes = lax.broadcasted_iota(jnp.int32, (sums.shape[0], 128), 1)
    return jnp.where(lanes < 64, high, sums - high).astype(BF16)


def join_lanes(terms):
    return terms + pltpu.roll(terms, 64, 1)


def silu(v):
    return v / (1.0 + jnp.exp(-v))


def kernel(
    order,
    tokens,
    norm_gain,
    w_z,
    w_x,
    w_bc,
    w_dt,
    conv_x,
    conv_bc,
    dt_bias,
    decay_rate,
    skip_gain,
    inner_gain,
    w_out,
    out,
    tokens_v,
    gain_v,
    next_gain,
    wz,
    wx,
    wbc,
    wdt,
    wout,
    cx,
    cbc,
    bias_v,
    rate_v,
    skip_v,
    inner_v,
    lhs,
    hop,
    held,
    sums_out,
    sums_in,
    fresh,
    ready,
    rows_in,
    x_hist,
    bc_hist,
    state,
    small_sem,
    weight_sem,
    gain_sem,
    lhs_send,
    lhs_recv,
    hop_send,
    hop_recv,
    held_send,
    held_recv,
    sums_send,
    sums_recv,
    rows_send,
    rows_recv,
):
    section = lax.axis_index("pipe")
    dp = lax.axis_index("dp")
    tensor = lax.axis_index("tensor")
    me = dp * 2 + tensor
    rb = lax.div(me, 4)
    fb = lax.rem(me, 4)
    my_x = tensor * 2 + lax.div(dp, 4)
    my_y = lax.rem(dp, 4)
    even = lax.rem(section, 2) == 0
    first = section == 0
    last = section == SECTIONS - 1

    def at_member(sec, member):
        return {"pipe": sec, "dp": lax.div(member, 2), "tensor": lax.rem(member, 2)}

    def at_offset(sec, d):
        x = lax.rem(my_x + lax.div(d, 4), 4)
        y = lax.rem(my_y + lax.rem(d, 4), 4)
        return {"pipe": sec, "dp": lax.rem(x, 2) * 4 + y, "tensor": lax.div(x, 2)}

    def remote(src, dst, send, recv, device):
        return pltpu.make_async_remote_copy(
            src_ref=src, dst_ref=dst, send_sem=send, recv_sem=recv, device_id=device, device_id_type=MESH
        )

    def wait_bytes(ref, sem):
        pltpu.make_async_copy(ref, ref, sem).wait()

    my_rows = pl.ds(pl.multiple_of(rb * ROWS, ROWS), ROWS)
    my_cols = pl.ds(pl.multiple_of(fb * COLS, COLS), COLS)

    small = [
        (conv_x.at[0], cx),
        (conv_bc.at[0], cbc),
        (dt_bias, bias_v),
        (decay_rate, rate_v),
        (skip_gain, skip_v),
        (inner_gain, inner_v),
        (norm_gain, gain_v),
    ]
    small_copies = [pltpu.make_async_copy(a, b, small_sem.at[i]) for i, (a, b) in enumerate(small)]
    token_copy = pltpu.make_async_copy(tokens, tokens_v, small_sem.at[len(small)])
    weights = [(w_dt, wdt), (w_bc, wbc), (w_x, wx), (w_z, wz), (w_out, wout)]
    weight_copies = [pltpu.make_async_copy(a.at[0], b, weight_sem.at[i]) for i, (a, b) in enumerate(weights)]
    for copy in small_copies:
        copy.start()

    @pl.when(first)
    def _():
        token_copy.start()

    for copy in weight_copies:
        copy.start()

    barrier = pltpu.get_barrier_semaphore()

    def greet(sec):
        def one(d, carry):
            pl.semaphore_signal(barrier, inc=1, device_id=at_offset(sec, d), device_id_type=MESH)
            return carry

        return one

    lax.fori_loop(1, MEMBERS, greet(section), 0)

    @pl.when(jnp.logical_not(even))
    def _():
        lax.fori_loop(0, MEMBERS, greet(section - 1), 0)

    @pl.when(jnp.logical_and(even, section > 0))
    def _():
        pl.semaphore_signal(barrier, inc=1, device_id=at_member(section - 1, me), device_id_type=MESH)

    @pl.when(section < SECTIONS - 1)
    def _():
        pl.semaphore_signal(barrier, inc=1, device_id=at_member(section + 1, me), device_id_type=MESH)

    x_hist[0:8, :] = jnp.zeros((8, INNER), F32)
    bc_hist[0:8, :] = jnp.zeros((8, 2 * STATE), F32)
    state[...] = jnp.zeros((STATE, INNER), F32)

    to_next = jnp.where(even, MEMBERS, jnp.where(last, 0, 1))
    to_previous = jnp.where(first, 0, 1)
    pl.semaphore_wait(barrier, MEMBERS - 1 + to_next + to_previous)

    gain_copy = remote(norm_gain, next_gain, gain_sem.at[0], gain_sem.at[1], at_member(section - 1, me))

    @pl.when(section > 0)
    def _():
        gain_copy.start()

    for copy in small_copies:
        copy.wait()

    @pl.when(first)
    def _():
        token_copy.wait()

    for copy in weight_copies:
        copy.wait()

    @pl.when(section < SECTIONS - 1)
    def _():
        gain_copy.wait_recv()

    def step(k, carry):
        @pl.when(first)
        def _():
            place = order[k]
            for f in range(4):
                part = tokens_v[place, :, f * COLS : (f + 1) * COLS].astype(F32)
                lhs[k, f, :, 0:COLS] = (part * gain_v[0:1, f * COLS : (f + 1) * COLS]).astype(BF16)
                lhs[k, f, :, COLS:WIDE] = split_lanes(jnp.sum(part * part, axis=1, keepdims=True))
            held[k] = tokens_v[place, my_rows, my_cols]

        @pl.when(section > 0)
        def _():
            @pl.when(even)
            def _():
                wait_bytes(hop.at[k], hop_recv.at[k])

                def forward(d, carry):
                    remote(
                        hop.at[k], lhs.at[k, fb, my_rows], lhs_send.at[k], lhs_recv.at[k], at_offset(section, d)
                    ).start()
                    return carry

                lax.fori_loop(1, MEMBERS, forward, 0)
                pltpu.make_async_copy(hop.at[k], lhs.at[k, fb, my_rows], lhs_recv.at[k]).start()

            wait_bytes(lhs.at[k], lhs_recv.at[k])

        sums = lhs[k, 0, :, COLS:WIDE].astype(F32)
        for f in range(1, 4):
            sums = sums + lhs[k, f, :, COLS:WIDE].astype(F32)
        scale = lax.rsqrt(join_lanes(sums) * (1.0 / WIDTH) + EPS)

        def project(weight):
            total = jnp.dot(lhs[k, 0, :, 0:COLS], weight[0:COLS], preferred_element_type=F32)
            for f in range(1, 4):
                total = total + jnp.dot(
                    lhs[k, f, :, 0:COLS], weight[f * COLS : (f + 1) * COLS], preferred_element_type=F32
                )
            return total

        dt_raw = project(wdt) * scale[:, 0:HEADS]
        bc_hist[8:72, :] = project(wbc) * jnp.concatenate([scale] * 2, axis=1)
        x_hist[8:72, :] = project(wx) * jnp.concatenate([scale] * 4, axis=1)
        gate_in = project(wz) * jnp.concatenate([scale] * 4, axis=1)

        bc_conv = cbc[0:1, :] * bc_hist[5:69, :]
        x_conv = cx[0:1, :] * x_hist[5:69, :]
        for j in range(1, CONV):
            bc_conv = bc_conv + cbc[j : j + 1, :] * bc_hist[5 + j : 69 + j, :]
            x_conv = x_conv + cx[j : j + 1, :] * x_hist[5 + j : 69 + j, :]
        bc_act = silu(bc_conv)
        x_act = silu(x_conv)
        b_part = bc_act[:, 0:STATE].astype(BF16)
        c_part = bc_act[:, STATE:].astype(BF16)

        raised = dt_raw + bias_v[...]
        steps = jnp.maximum(raised, 0.0) + jnp.log1p(jnp.exp(-jnp.abs(raised)))
        t64 = lax.broadcasted_iota(jnp.int32, (LENGTH, LENGTH), 0)
        s64 = lax.broadcasted_iota(jnp.int32, (LENGTH, LENGTH), 1)
        lower = (t64 >= s64).astype(F32)
        cumulated = jnp.dot(lower, -steps * rate_v[...], precision=HIGH, preferred_element_type=F32)
        spread = (
            lax.div(lax.broadcasted_iota(jnp.int32, (HEADS, INNER), 1), HEAD_DIM)
            == lax.broadcasted_iota(jnp.int32, (HEADS, INNER), 0)
        ).astype(F32)
        cum_wide = jnp.dot(cumulated, spread, precision=HIGH, preferred_element_type=F32)
        step_wide = jnp.dot(steps, spread, precision=HIGH, preferred_element_type=F32)
        skip_wide = jnp.dot(skip_v[...], spread, precision=HIGH, preferred_element_type=F32)
        t_wide = lax.broadcasted_iota(jnp.int32, (LENGTH, INNER), 0)
        s_wide = lax.rem(lax.broadcasted_iota(jnp.int32, (LENGTH, INNER), 1), HEAD_DIM)
        on_diag = t_wide == s_wide
        cum_row = jnp.sum(jnp.where(on_diag, cum_wide, 0.0), axis=0, keepdims=True)
        step_row = jnp.sum(jnp.where(on_diag, step_wide, 0.0), axis=0, keepdims=True)
        decays = jnp.exp(jnp.where(t_wide >= s_wide, cum_wide - cum_row, -1e30)) * step_row

        scores = lax.dot_general(
            c_part,
            jnp.concatenate([b_part, b_part], axis=0),
            (((1,), (1,)), ((), ())),
            preferred_element_type=F32,
        )
        lanes = lax.broadcasted_iota(jnp.int32, (LENGTH, 128), 1)
        carried = jnp.dot(c_part, state[...].astype(BF16), preferred_element_type=F32)
        y = jnp.exp(cum_wide) * carried + skip_wide * x_act
        inside = []
        for j in range(4):
            cols = slice(128 * j, 128 * (j + 1))
            x_pair = x_act[:, cols]
            block = jnp.concatenate(
                [jnp.where(lanes < 64, x_pair, 0.0), jnp.where(lanes < 64, 0.0, x_pair)], axis=0
            ).astype(BF16)
            inside.append(jnp.dot((scores * decays[:, cols]).astype(BF16), block, preferred_element_type=F32))
        y = y + jnp.concatenate(inside, axis=1)

        gated = y * silu(gate_in)
        squares = split_lanes(jnp.sum(gated * gated, axis=1, keepdims=True))
        mixed = (gated * inner_v[...]).astype(BF16)

        for j in range(4):
            f = lax.rem(fb + 1 + j, 4)
            part = jnp.dot(
                mixed, wout[:, pl.ds(pl.multiple_of(f * COLS, COLS), COLS)], preferred_element_type=F32
            )
            sums_out[k, f, :, 0:COLS] = part.astype(BF16)
            sums_out[k, f, :, COLS:WIDE] = squares
            for i in range(4):
                r = lax.rem(rb + 1 + i, 4)
                block = sums_out.at[k, f, pl.ds(pl.multiple_of(r * ROWS, ROWS), ROWS)]
                if j == 3 and i == 3:
                    pltpu.make_async_copy(block, sums_in.at[k, me], sums_recv.at[k]).start()
                else:
                    remote(
                        block, sums_in.at[k, me], sums_send.at[k], sums_recv.at[k], at_member(section, r * 4 + f)
                    ).start()

        last_cum = cum_wide[LENGTH - 1 : LENGTH, :]
        remaining = x_act * (jnp.exp(last_cum - cum_wide) * step_wide)
        state[...] = jnp.exp(last_cum) * state[...] + lax.dot_general(
            b_part, remaining.astype(BF16), (((0,), (0,)), ((), ())), preferred_element_type=F32
        )
        x_hist[0:8, :] = x_hist[64:72, :]
        bc_hist[0:8, :] = bc_hist[64:72, :]

        @pl.when(section > 0)
        def _():
            wait_bytes(held.at[k], held_recv.at[k])

        wait_bytes(sums_in.at[k], sums_recv.at[k])
        total = held[k].astype(F32)
        for g in range(8):
            one, two = sums_in.at[k, 2 * g], sums_in.at[k, 2 * g + 1]
            sq = join_lanes(one[:, COLS:WIDE].astype(F32) + two[:, COLS:WIDE].astype(F32))
            factor = lax.rsqrt(sq * (1.0 / CHANNELS) + EPS)
            both = one[:, 0:COLS].astype(F32) + two[:, 0:COLS].astype(F32)
            total = total + both * jnp.concatenate([factor] * (COLS // 128), axis=1)
        updated = total.astype(BF16)
        fresh[k] = updated

        @pl.when(section < SECTIONS - 1)
        def _():
            value = updated.astype(F32)
            ready[k, :, 0:COLS] = (value * next_gain[0:1, my_cols]).astype(BF16)
            ready[k, :, COLS:WIDE] = split_lanes(jnp.sum(value * value, axis=1, keepdims=True))

            @pl.when(even)
            def _():
                def spread_out(d, carry):
                    remote(
                        ready.at[k],
                        lhs.at[k, fb, my_rows],
                        lhs_send.at[k],
                        lhs_recv.at[k],
                        at_offset(section + 1, d),
                    ).start()
                    return carry

                lax.fori_loop(0, MEMBERS, spread_out, 0)

            @pl.when(jnp.logical_not(even))
            def _():
                remote(
                    ready.at[k], hop.at[k], hop_send.at[k], hop_recv.at[k], at_member(section + 1, me)
                ).start()

            remote(
                fresh.at[k], held.at[k], held_send.at[k], held_recv.at[k], at_member(section + 1, me)
            ).start()

        for i in range(1, 4):
            remote(
                fresh.at[k],
                rows_in.at[k, fb],
                rows_send.at[k],
                rows_recv.at[k],
                at_member(section, rb * 4 + lax.rem(fb + i, 4)),
            ).start()
        pltpu.make_async_copy(fresh.at[k], rows_in.at[k, fb], rows_recv.at[k]).start()
        return carry

    lax.fori_loop(0, SLICES, step, 0)

    pick = (
        lax.broadcasted_iota(jnp.int32, (8, ROWS), 1) == lax.broadcasted_iota(jnp.int32, (8, ROWS), 0) + 4 * fb
    ).astype(BF16)
    for k in range(SLICES):
        wait_bytes(rows_in.at[k], rows_recv.at[k])
        for f in range(4):
            chosen = jnp.dot(pick, rows_in[k, f], preferred_element_type=F32)
            out[0, k, :, f * COLS : (f + 1) * COLS] = chosen[0:4].astype(BF16)

    def drain(k, carry):
        wait_bytes(sums_in.at[k, pl.ds(0, MEMBERS - 1)], sums_send.at[k])
        wait_bytes(rows_in.at[k, pl.ds(0, 3)], rows_send.at[k])

        @pl.when(section < SECTIONS - 1)
        def _():
            wait_bytes(held.at[k], held_send.at[k])

            @pl.when(jnp.logical_not(even))
            def _():
                wait_bytes(hop.at[k], hop_send.at[k])

        @pl.when(even)
        def _():
            wait_bytes(sums_in.at[k], lhs_send.at[k])

            @pl.when(section > 0)
            def _():
                wait_bytes(sums_in.at[k, pl.ds(0, MEMBERS - 1)], lhs_send.at[k])

        return carry

    lax.fori_loop(0, SLICES, drain, 0)

    @pl.when(section > 0)
    def _():
        gain_copy.wait_send()


def local(tokens, slice_order, *rest):
    hbm = pl.BlockSpec(memory_space=pltpu.HBM)
    dma = pltpu.SemaphoreType.DMA
    return pl.pallas_call(
        kernel,
        out_shape=jax.ShapeDtypeStruct((1, SLICES, LENGTH // MEMBERS, WIDTH), BF16),
        in_specs=[pl.BlockSpec(memory_space=pltpu.SMEM)] + [hbm] * (1 + len(rest)),
        out_specs=pl.BlockSpec(memory_space=pltpu.VMEM),
        scratch_shapes=[
            pltpu.VMEM((SLICES, LENGTH, WIDTH), BF16),
            pltpu.VMEM((1, WIDTH), F32),
            pltpu.VMEM((1, WIDTH), F32),
            pltpu.VMEM((WIDTH, INNER), BF16),
            pltpu.VMEM((WIDTH, INNER), BF16),
            pltpu.VMEM((WIDTH, 2 * STATE), BF16),
            pltpu.VMEM((WIDTH, HEADS), BF16),
            pltpu.VMEM((INNER, WIDTH), BF16),
            pltpu.VMEM((CONV, INNER), F32),
            pltpu.VMEM((CONV, 2 * STATE), F32),
            pltpu.VMEM((1, HEADS), F32),
            pltpu.VMEM((1, HEADS), F32),
            pltpu.VMEM((1, HEADS), F32),
            pltpu.VMEM((1, INNER), F32),
            pltpu.VMEM((SLICES, 4, LENGTH, WIDE), BF16),
            pltpu.VMEM((SLICES, ROWS, WIDE), BF16),
            pltpu.VMEM((SLICES, ROWS, COLS), BF16),
            pltpu.VMEM((SLICES, 4, LENGTH, WIDE), BF16),
            pltpu.VMEM((SLICES, MEMBERS, ROWS, WIDE), BF16),
            pltpu.VMEM((SLICES, ROWS, COLS), BF16),
            pltpu.VMEM((SLICES, ROWS, WIDE), BF16),
            pltpu.VMEM((SLICES, 4, ROWS, COLS), BF16),
            pltpu.VMEM((LENGTH + 8, INNER), F32),
            pltpu.VMEM((LENGTH + 8, 2 * STATE), F32),
            pltpu.VMEM((STATE, INNER), F32),
            dma((8,)),
            dma((5,)),
            dma((2,)),
            dma((SLICES,)),
            dma((SLICES,)),
            dma((SLICES,)),
            dma((SLICES,)),
            dma((SLICES,)),
            dma((SLICES,)),
            dma((SLICES,)),
            dma((SLICES,)),
            dma((SLICES,)),
            dma((SLICES,)),
        ],
        compiler_params=pltpu.CompilerParams(
            collective_id=0, has_side_effects=True, vmem_limit_bytes=48 * 1024 * 1024
        ),
    )(slice_order, tokens, *rest)


def solution(mesh):
    both = ("dp", "tensor")
    placed = (
        P(),
        P(),
        P("pipe", None),
        P("pipe", None, both),
        P("pipe", None, both),
        P("pipe", None, "dp"),
        P("pipe", None, both),
        P("pipe", None, both),
        P("pipe", None, "dp"),
        P("pipe", both),
        P("pipe", both),
        P("pipe", both),
        P("pipe", both),
        P("pipe", both, None),
    )
    return jax.shard_map(
        local,
        mesh=mesh,
        in_specs=placed,
        out_specs=P("pipe", None, both, None),
        check_vma=False,
    )
```

time: 1430 us -> 229 us (0.16)
  waiting for transfers between devices: 1160 us -> 0 us
  Pallas kernels: 0 us -> 217 us
  matrix products: 66.3 us -> 0 us
  blocking collectives: 58.1 us -> 0 us
  other arithmetic: 40.6 us -> 0 us
  local copies, waits for them, and re-layouts: 39 us -> 10.5 us
  loops' own time: 23.5 us -> 0 us
  starting transfers between devices: 14.3 us -> 0 us
    psum x11 -> x0, waiting for transfers between devices: 1120 us -> none  [tick(): summed = lax.psum(terms, ('dp', 'tensor'))]
    pallas_call x0 -> x1, Pallas kernels: none -> 217 us  [local(): pl.pallas_call(kernel, out_shape=jax.ShapeDtypeStruct((1, SLICES, LENGTH...]
    dot_general x40 -> x0, matrix products: 66.3 us -> none  [the longest x4 15.1 us: mixer_part(): gate_in = jnp.dot(normed, w_z, preferred_element_type=jnp.float32)]
    psum x11 -> x0, blocking collectives: 58.1 us -> none  [tick(): totals = lax.psum(squares, 'tensor')]
    ppermute x11 -> x0, waiting for transfers between devices: 45.6 us -> none  [shifted(): lax.ppermute(value, axis, [(source, source + steps) for source in range(l...]
    convert_element_type x34 -> x0, other arithmetic: 25.6 us -> none  [the longest x11 14.4 us: tick(): updated = (current.astype(jnp.float32) + summed).astype(jnp.bfloat16)]
    another operation x23 -> x0, loops' own time: 23.5 us -> none  [the longest x1 22.4 us: local(): final_carry = lax.fori_loop(0, ticks, tick, start_carry)]
  transfers between devices with their start and end apart: 22 -> 0, of which waited for: 22 -> 0; matrix products, arithmetic and copies ran while one was open for 0% -> 0% of each run, Pallas kernels for 0% -> 0%
where the time goes in v1:
time: 229 us; the launch traced here: 228 us
  Pallas kernels  217 us (95%)
  local copies, waits for them, and re-layouts  10.5 us (5%)
    pallas_call x1, Pallas kernels, local(): pl.pallas_call(kernel, out_shape=jax.ShapeDtypeStruct((1, SLICES, LENGTH...  217 us
    unnamed x22, local copies, waits for them, and re-layouts  10.5 us

profile of v1, /device:TPU:99, one launch (start us, length us, event | category | flops | bytes accessed | tf_op | source)
XLA Modules:
  0.0 227.8 jit_solution(17151786717473296247)
XLA Ops:
  0.0 1.3 copy.15.w_dt
  1.3 0.0 copy-start
  1.3 1.6 copy-done
  2.9 0.0 copy-start.1
  2.9 1.6 copy-done.1
  4.5 0.0 copy-start.2
  4.5 0.7 copy-done.2
  5.2 0.0 copy-start.3
  5.2 0.7 copy-done.3
  5.9 0.0 copy-start.4
  5.9 0.7 copy-done.4
  6.6 0.0 copy-start.5
  6.6 0.7 copy-done.5
  7.3 0.0 copy-start.6
  7.3 0.7 copy-done.6
  7.9 0.0 copy-start.7
  7.9 0.7 copy-done.7
  8.6 0.0 copy-start.8
  8.6 0.7 copy-done.8
  9.3 0.0 copy-start.9
  9.3 0.7 copy-done.9
  9.9 217.2 %shard_map.136 = bf16[1,4,4,4096]{3,2,1,0:T(4,128)(2,1)S(1)} custom-call(s32[4]{0:T(128)S(1)} %copy-done.6, bf16[4,64,4096]{2,1,0:T(8,128)(2,1)S(1)} %copy-done, f32[1,4096]{1,0:T(1,128)S(1)} %copy-done.2, bf16[1,4096,512]{2,1,0:T(8,128)(2,1)} %w_z.1, bf16[1,4096,512]{2,1,0:T(8,128)(2,1)} %w_x.1, bf16[1,4096,256]{2,1,0:T(8,128)(2,1)S(1)} %copy-done.1, ...), custom_call_target="tpu_custom_call" | custom-call | tf_op jit(solution)/shard_map/pallas_call | solution.py:428
  227.1 0.7 copy.17
Async XLA Ops:
  1.3 1.6 copy-start
  2.9 1.6 copy-start.1
  4.5 0.7 copy-start.2
  5.2 0.7 copy-start.3
  5.9 0.7 copy-start.4
  6.6 0.7 copy-start.5
  7.3 0.7 copy-start.6
  7.9 0.7 copy-start.7
  8.6 0.7 copy-start.8
  9.3 0.7 copy-start.9

commit v2 on v1

v2 whole, which is shorter than its diff:
```python
import jax
import jax.numpy as jnp
from jax import lax
from jax.experimental import pallas as pl
from jax.experimental.pallas import tpu as pltpu
from jax.sharding import PartitionSpec as P

MESH = pl.DeviceIdType.MESH
F32 = jnp.float32
BF16 = jnp.bfloat16
EPS = 1e-05
HIGH = lax.Precision.HIGHEST

SECTIONS = 8
MEMBERS = 16
SLICES = 4
SLICE = 64
LENGTH = 32
PIECES = SLICES * SLICE // LENGTH
SKEW = 1
WIDTH = 4096
OWN = WIDTH // MEMBERS
STATE = 128
CONV = 4
HEADS = 8
HEAD_DIM = 64
INNER = HEADS * HEAD_DIM
CHANNELS = 1024
BD = 2 * STATE + 128
SENT = 2 * OWN + 128
GROUPS_IN = 2


def ring_distance(step):
    return min(step, 4 - step)


OFFSETS = sorted(
    [(dx, dy) for dx in range(4) for dy in range(4)],
    key=lambda o: -(ring_distance(o[0]) + ring_distance(o[1])),
)


def silu(v):
    return v / (1.0 + jnp.exp(-v))


def kernel(
    order,
    tokens,
    norm_gain,
    w_z,
    w_x,
    w_bc,
    w_dt,
    conv_x,
    conv_bc,
    dt_bias,
    decay_rate,
    skip_gain,
    inner_gain,
    w_out,
    out,
    tokens_v,
    gain_v,
    wz,
    wx,
    wbd,
    wdt,
    wout,
    cx,
    cbc,
    bias_v,
    rate_v,
    skip_v,
    inner_v,
    lhs,
    sums_out,
    sums_in,
    fresh,
    rows_out,
    x_hist,
    bc_hist,
    state,
    small_sem,
    weight_sem,
    out_sem,
    lhs_send,
    lhs_recv,
    sums_send,
    sums_recv,
    rows_send,
    rows_recv,
):
    section = lax.axis_index("pipe")
    dp = lax.axis_index("dp")
    tensor = lax.axis_index("tensor")
    me = dp * 2 + tensor
    my_x = tensor * 2 + lax.div(dp, 4)
    my_y = lax.rem(dp, 4)
    first = section == 0
    last = section == SECTIONS - 1

    def member(dx, dy):
        x, y = lax.rem(my_x + dx, 4), lax.rem(my_y + dy, 4)
        return (lax.rem(x, 2) * 4 + y) * 2 + lax.div(x, 2)

    def device(sec, m):
        return {"pipe": sec, "dp": lax.div(m, 2), "tensor": lax.rem(m, 2)}

    targets = [member(dx, dy) for dx, dy in OFFSETS]
    sources = [member(4 - dx, 4 - dy) for dx, dy in OFFSETS]

    def remote(src, dst, send, recv, sec, m):
        return pltpu.make_async_remote_copy(
            src_ref=src, dst_ref=dst, send_sem=send, recv_sem=recv, device_id=device(sec, m), device_id_type=MESH
        )

    def wait_bytes(ref, sem):
        pltpu.make_async_copy(ref, ref, sem).wait()

    small = [
        (norm_gain, gain_v),
        (w_dt.at[0], wdt),
        (conv_x.at[0], cx),
        (conv_bc.at[0], cbc),
        (dt_bias, bias_v),
        (decay_rate, rate_v),
        (skip_gain, skip_v),
        (inner_gain, inner_v),
    ]
    small_copies = [pltpu.make_async_copy(a, b, small_sem.at[i]) for i, (a, b) in enumerate(small)]
    token_copy = pltpu.make_async_copy(tokens, tokens_v, small_sem.at[len(small)])
    for copy in small_copies:
        copy.start()

    def weight_copies(c):
        rows = pl.ds(pl.multiple_of(c * OWN, OWN), OWN)
        return [
            pltpu.make_async_copy(w_bc.at[0, rows], wbd.at[rows, 0 : 2 * STATE], weight_sem.at[c, 0]),
            pltpu.make_async_copy(w_x.at[0, rows], wx.at[rows], weight_sem.at[c, 1]),
            pltpu.make_async_copy(w_z.at[0, rows], wz.at[rows], weight_sem.at[c, 2]),
        ]

    def out_copy(c):
        cols = pl.ds(pl.multiple_of(c * OWN, OWN), OWN)
        return pltpu.make_async_copy(w_out.at[0, :, cols], wout.at[c], out_sem.at[c])

    def load(c, carry):
        for copy in weight_copies(c):
            copy.start()
        return carry

    def load_out(c, carry):
        out_copy(c).start()
        return carry

    lax.fori_loop(0, MEMBERS, load, 0)

    @pl.when(first)
    def _():
        token_copy.start()

    lax.fori_loop(0, MEMBERS, load_out, 0)

    barrier = pltpu.get_barrier_semaphore()

    def greet(sec, members):
        for m in members:
            pl.semaphore_signal(barrier, inc=1, device_id=device(sec, m), device_id_type=MESH)

    greet(section, sources[:-1])

    @pl.when(section > 0)
    def _():
        greet(section - 1, sources)

    x_hist[0:8, :] = jnp.zeros((8, INNER), F32)
    bc_hist[0:8, :] = jnp.zeros((8, 2 * STATE), F32)
    state[...] = jnp.zeros((STATE, INNER), F32)
    for copy in small_copies:
        copy.wait()

    diagonal = lax.broadcasted_iota(jnp.int32, (OWN, OWN), 0) == lax.broadcasted_iota(jnp.int32, (OWN, OWN), 1)

    def fold(c, carry):
        rows = pl.ds(pl.multiple_of(c * OWN, OWN), OWN)
        along = gain_v[0:1, rows]
        down = jnp.sum(jnp.where(diagonal, along, 0.0), axis=1, keepdims=True)
        steps = jnp.concatenate([wdt[:, rows].astype(F32) * along, jnp.zeros((128 - HEADS, OWN), F32)], axis=0)
        wbd[rows, 2 * STATE : BD] = jnp.transpose(steps).astype(BF16)
        for copy in weight_copies(c):
            copy.wait()
        wbd[rows, 0 : 2 * STATE] = (wbd[rows, 0 : 2 * STATE].astype(F32) * down).astype(BF16)
        wx[rows, :] = (wx[rows, :].astype(F32) * down).astype(BF16)
        wz[rows, :] = (wz[rows, :].astype(F32) * down).astype(BF16)
        return carry

    lax.fori_loop(0, MEMBERS, fold, 0)

    @pl.when(first)
    def _():
        token_copy.wait()

    pl.semaphore_wait(barrier, MEMBERS - 1 + jnp.where(last, 0, MEMBERS))

    def load_out_wait(c, carry):
        out_copy(c).wait()
        return carry

    lax.fori_loop(0, MEMBERS, load_out_wait, 0)

    spread = (
        lax.div(lax.broadcasted_iota(jnp.int32, (HEADS, INNER), 1), HEAD_DIM)
        == lax.broadcasted_iota(jnp.int32, (HEADS, INNER), 0)
    ).astype(F32)
    spread_rows = (
        lax.div(lax.broadcasted_iota(jnp.int32, (HEADS, HEADS * LENGTH), 1), LENGTH)
        == lax.broadcasted_iota(jnp.int32, (HEADS, HEADS * LENGTH), 0)
    ).astype(F32)
    skip_wide = jnp.dot(skip_v[...], spread, precision=HIGH, preferred_element_type=F32)

    def front(k):
        @pl.when(first)
        def _():
            place = order[lax.div(k, 2)]
            rows = pl.ds(pl.multiple_of(lax.rem(k, 2) * LENGTH, LENGTH), LENGTH)
            for c in range(MEMBERS):
                lhs[k, c] = tokens_v[place, rows, c * OWN : (c + 1) * OWN]

        bd_sum = jnp.zeros((LENGTH, BD), F32)
        x_sum = jnp.zeros((LENGTH, INNER), F32)
        squares = jnp.zeros((LENGTH, OWN), F32)
        per_group = MEMBERS // GROUPS_IN
        for g in range(GROUPS_IN):

            @pl.when(section > 0)
            def _():
                wait_bytes(lhs.at[k, pl.ds(0, per_group)], lhs_recv.at[k, g])

            for i in range(g * per_group, (g + 1) * per_group):
                c = sources[i]
                rows = pl.ds(pl.multiple_of(c * OWN, OWN), OWN)
                block = lhs[k, c]
                bd_sum = bd_sum + jnp.dot(block, wbd[rows, :], preferred_element_type=F32)
                x_sum = x_sum + jnp.dot(block, wx[rows, :], preferred_element_type=F32)
                wide = block.astype(F32)
                squares = squares + wide * wide
        scale = lax.rsqrt(jnp.sum(squares, axis=1, keepdims=True) * (1.0 / WIDTH) + EPS)
        dt_raw = bd_sum[:, 2 * STATE : 2 * STATE + HEADS] * scale
        bc_hist[8 : LENGTH + 8, :] = bd_sum[:, 0 : 2 * STATE] * scale
        x_hist[8 : LENGTH + 8, :] = x_sum * scale

        bc_conv = cbc[0:1, :] * bc_hist[5 : LENGTH + 5, :]
        x_conv = cx[0:1, :] * x_hist[5 : LENGTH + 5, :]
        for j in range(1, CONV):
            bc_conv = bc_conv + cbc[j : j + 1, :] * bc_hist[5 + j : LENGTH + 5 + j, :]
            x_conv = x_conv + cx[j : j + 1, :] * x_hist[5 + j : LENGTH + 5 + j, :]
        bc_act = silu(bc_conv)
        x_act = silu(x_conv)
        b_part = bc_act[:, 0:STATE].astype(BF16)
        c_part = bc_act[:, STATE:].astype(BF16)

        raised = dt_raw + bias_v[...]
        steps = jnp.maximum(raised, 0.0) + jnp.log1p(jnp.exp(-jnp.abs(raised)))
        lower = (
            lax.broadcasted_iota(jnp.int32, (LENGTH, LENGTH), 0)
            >= lax.broadcasted_iota(jnp.int32, (LENGTH, LENGTH), 1)
        ).astype(F32)
        cumulated = jnp.dot(lower, -steps * rate_v[...], precision=HIGH, preferred_element_type=F32)
        ending = cumulated[LENGTH - 1 : LENGTH, :]
        cum_rows = jnp.dot(cumulated, spread_rows, precision=HIGH, preferred_element_type=F32)
        step_rows = jnp.dot(steps, spread_rows, precision=HIGH, preferred_element_type=F32)
        grown = jnp.dot(jnp.exp(cumulated), spread, precision=HIGH, preferred_element_type=F32)
        remains = jnp.dot(jnp.exp(ending - cumulated) * steps, spread, precision=HIGH, preferred_element_type=F32)
        t_wide = lax.broadcasted_iota(jnp.int32, (LENGTH, HEADS * LENGTH), 0)
        s_wide = lax.rem(lax.broadcasted_iota(jnp.int32, (LENGTH, HEADS * LENGTH), 1), LENGTH)
        on_diag = t_wide == s_wide
        cum_row = jnp.sum(jnp.where(on_diag, cum_rows, 0.0), axis=0, keepdims=True)
        step_row = jnp.sum(jnp.where(on_diag, step_rows, 0.0), axis=0, keepdims=True)
        decays = jnp.exp(jnp.where(t_wide >= s_wide, cum_rows - cum_row, -1e30)) * step_row

        scores = lax.dot_general(
            c_part, jnp.concatenate([b_part] * 4, axis=0), (((1,), (1,)), ((), ())), preferred_element_type=F32
        )
        weighted = (jnp.concatenate([scores] * 2, axis=1) * decays).astype(BF16)
        low = lax.broadcasted_iota(jnp.int32, (LENGTH, 128), 1) < HEAD_DIM
        blocks = []
        for h in range(HEADS):
            pair = x_act[:, 128 * (h // 2) : 128 * (h // 2 + 1)]
            mine = jnp.where(low, pair, 0.0) if h % 2 == 0 else jnp.where(low, 0.0, pair)
            parts = [mine if j == h // 2 else jnp.zeros((LENGTH, 128), F32) for j in range(HEADS // 2)]
            blocks.append(jnp.concatenate(parts, axis=1))
        inside = jnp.dot(weighted, jnp.concatenate(blocks, axis=0).astype(BF16), preferred_element_type=F32)
        carried = jnp.dot(c_part, state[...].astype(BF16), preferred_element_type=F32)
        y = inside + grown * carried + skip_wide * x_act

        z_sum = jnp.zeros((LENGTH, INNER), F32)
        for c in range(MEMBERS):
            z_sum = z_sum + jnp.dot(lhs[k, c], wz[c * OWN : (c + 1) * OWN, :], preferred_element_type=F32)
        gated = y * silu(z_sum * scale)
        mixed = (gated * inner_v[...]).astype(BF16)

        total = jnp.sum(gated * gated, axis=1, keepdims=True)
        high = total.astype(BF16).astype(F32)
        lane = lax.broadcasted_iota(jnp.int32, (16, 128), 1)
        even = lax.rem(lax.div(lane, 32), 2) == 0
        terms = jnp.where(
            lane < 64,
            jnp.where(even, high[0:16], high[16:32]),
            jnp.where(even, (total - high)[0:16], (total - high)[16:32]),
        ).astype(BF16)

        for i in range(MEMBERS):
            m = targets[i]
            part = jnp.dot(mixed, wout[m], preferred_element_type=F32).astype(BF16)
            sums_out[k, m, :, 0:OWN] = part[0:16]
            sums_out[k, m, :, OWN : 2 * OWN] = part[16:32]
            sums_out[k, m, :, 2 * OWN : SENT] = terms
            if i < MEMBERS - 1:
                remote(
                    sums_out.at[k, m], sums_in.at[k, me], sums_send.at[k], sums_recv.at[k], section, m
                ).start()
            else:
                pltpu.make_async_copy(sums_out.at[k, m], sums_in.at[k, me], sums_recv.at[k]).start()

        state[...] = grown[LENGTH - 1 : LENGTH, :] * state[...] + lax.dot_general(
            b_part, (x_act * remains).astype(BF16), (((0,), (0,)), ((), ())), preferred_element_type=F32
        )
        x_hist[0:8, :] = x_hist[LENGTH : LENGTH + 8, :]
        bc_hist[0:8, :] = bc_hist[LENGTH : LENGTH + 8, :]

    def back(k):
        wait_bytes(sums_in.at[k], sums_recv.at[k])
        lane = lax.broadcasted_iota(jnp.int32, (16, 128), 1)
        even = lax.rem(lax.div(lane, 32), 2) == 0
        held = lhs[k, me].astype(F32)
        upper, lower = held[0:16], held[16:32]
        for g in range(MEMBERS // 2):
            both = sums_in[k, 2 * g].astype(F32) + sums_in[k, 2 * g + 1].astype(F32)
            sq = both[:, 2 * OWN : SENT]
            sq = sq + pltpu.roll(sq, 64, 1)
            factor = lax.rsqrt(sq * (1.0 / CHANNELS) + EPS)
            other = pltpu.roll(factor, 32, 1)
            top, bottom = jnp.where(even, factor, other), jnp.where(even, other, factor)
            upper = upper + both[:, 0:OWN] * jnp.concatenate([top] * 2, axis=1)
            lower = lower + both[:, OWN : 2 * OWN] * jnp.concatenate([bottom] * 2, axis=1)
        fresh[k, 0:16, :] = upper.astype(BF16)
        fresh[k, 16:32, :] = lower.astype(BF16)

        @pl.when(section < SECTIONS - 1)
        def _():
            for i in range(MEMBERS):
                remote(
                    fresh.at[k],
                    lhs.at[k, me],
                    lhs_send.at[k],
                    lhs_recv.at[k, i // (MEMBERS // GROUPS_IN)],
                    section + 1,
                    targets[i],
                ).start()

    def step(i, carry):
        @pl.when(i < PIECES)
        def _():
            front(i)

        @pl.when(i >= SKEW)
        def _():
            back(i - SKEW)

        return carry

    lax.fori_loop(0, PIECES + SKEW, step, 0)

    for q in range(4):
        quad = jnp.concatenate(
            [fresh[2 * s + q // 2, 16 * (q % 2) : 16 * (q % 2) + 16, :] for s in range(SLICES)], axis=0
        )
        for i in range(4):
            to = lax.broadcasted_iota(jnp.int32, (16, 64), 0)
            of = lax.broadcasted_iota(jnp.int32, (16, 64), 1)
            pick = (of == lax.div(to, 4) * 16 + lax.rem(to, 4) + 4 * i).astype(BF16)
            rows_out[4 * q + i] = jnp.dot(pick, quad, preferred_element_type=F32).astype(BF16)
    mine = out.at[:, pl.ds(pl.multiple_of(me * OWN, OWN), OWN)]
    for i in range(MEMBERS):
        m = targets[i]
        if i < MEMBERS - 1:
            remote(rows_out.at[m], mine, rows_send.at[0], rows_recv.at[0], section, m).start()
        else:
            pltpu.make_async_copy(rows_out.at[m], mine, rows_recv.at[0]).start()

    def drain(k, carry):
        wait_bytes(sums_in.at[k, pl.ds(0, MEMBERS - 1)], sums_send.at[k])

        @pl.when(section < SECTIONS - 1)
        def _():
            wait_bytes(lhs.at[k], lhs_send.at[k])

        return carry

    lax.fori_loop(0, PIECES, drain, 0)
    wait_bytes(rows_out.at[pl.ds(0, MEMBERS - 1)], rows_send.at[0])
    wait_bytes(rows_out, rows_recv.at[0])


def local(tokens, slice_order, norm_gain, w_z, w_x, w_bc, w_dt, *rest):
    hbm = pl.BlockSpec(memory_space=pltpu.HBM)
    dma = pltpu.SemaphoreType.DMA
    args = (tokens, norm_gain, w_z, w_x, w_bc, jnp.swapaxes(w_dt, 1, 2), *rest)
    rows = pl.pallas_call(
        kernel,
        out_shape=jax.ShapeDtypeStruct((SLICES * SLICE // MEMBERS, WIDTH), BF16),
        in_specs=[pl.BlockSpec(memory_space=pltpu.SMEM)] + [hbm] * len(args),
        out_specs=pl.BlockSpec(memory_space=pltpu.VMEM),
        scratch_shapes=[
            pltpu.VMEM((SLICES, SLICE, WIDTH), BF16),
            pltpu.VMEM((1, WIDTH), F32),
            pltpu.VMEM((WIDTH, INNER), BF16),
            pltpu.VMEM((WIDTH, INNER), BF16),
            pltpu.VMEM((WIDTH, BD), BF16),
            pltpu.VMEM((HEADS, WIDTH), BF16),
            pltpu.VMEM((MEMBERS, INNER, OWN), BF16),
            pltpu.VMEM((CONV, INNER), F32),
            pltpu.VMEM((CONV, 2 * STATE), F32),
            pltpu.VMEM((1, HEADS), F32),
            pltpu.VMEM((1, HEADS), F32),
            pltpu.VMEM((1, HEADS), F32),
            pltpu.VMEM((1, INNER), F32),
            pltpu.VMEM((PIECES, MEMBERS, LENGTH, OWN), BF16),
            pltpu.VMEM((PIECES, MEMBERS, 16, SENT), BF16),
            pltpu.VMEM((PIECES, MEMBERS, 16, SENT), BF16),
            pltpu.VMEM((PIECES, LENGTH, OWN), BF16),
            pltpu.VMEM((MEMBERS, 16, OWN), BF16),
            pltpu.VMEM((LENGTH + 8, INNER), F32),
            pltpu.VMEM((LENGTH + 8, 2 * STATE), F32),
            pltpu.VMEM((STATE, INNER), F32),
            dma((9,)),
            dma((MEMBERS, 3)),
            dma((MEMBERS,)),
            dma((PIECES,)),
            dma((PIECES, GROUPS_IN)),
            dma((PIECES,)),
            dma((PIECES,)),
            dma((1,)),
            dma((1,)),
        ],
        compiler_params=pltpu.CompilerParams(
            collective_id=0, has_side_effects=True, vmem_limit_bytes=60 * 1024 * 1024
        ),
    )(slice_order, *args)
    return rows.reshape(1, SLICES, SLICE // MEMBERS, WIDTH)


def solution(mesh):
    both = ("dp", "tensor")
    placed = (
        P(),
        P(),
        P("pipe", None),
        P("pipe", None, both),
        P("pipe", None, both),
        P("pipe", None, "dp"),
        P("pipe", None, both),
        P("pipe", None, both),
        P("pipe", None, "dp"),
        P("pipe", both),
        P("pipe", both),
        P("pipe", both),
        P("pipe", both),
        P("pipe", both, None),
    )
    return jax.shard_map(
        local,
        mesh=mesh,
        in_specs=placed,
        out_specs=P("pipe", None, both, None),
        check_vma=False,
    )
```

time: 229 us -> 201 us (0.88)
  Pallas kernels: 217 us -> 198 us
  local copies, waits for them, and re-layouts: 10.5 us -> 1.62 us
    pallas_call x1, Pallas kernels: 217 us -> 198 us  [local(): pl.pallas_call(kernel, out_shape=jax.ShapeDtypeStruct((SLICES * SLICE //...]
    unnamed x22 -> x0, local copies, waits for them, and re-layouts: 10.5 us -> none
where the time goes in v2:
time: 201 us; the launch traced here: 200 us
  Pallas kernels  198 us (99%)
    pallas_call x1, Pallas kernels, local(): pl.pallas_call(kernel, out_shape=jax.ShapeDtypeStruct((SLICES * SLICE //...  198 us

profile of v2, /device:TPU:99, one launch (start us, length us, event | category | flops | bytes accessed | tf_op | source)
XLA Modules:
  0.0 200.1 jit_solution(10083118135894914231)
XLA Ops:
  0.0 198.5 %shard_map.136 = bf16[16,4096]{1,0:T(8,128)(2,1)} custom-call(s32[4]{0:T(128)} %order.1, bf16[4,64,4096]{2,1,0:T(8,128)(2,1)} %tokens.1, f32[1,4096]{1,0:T(1,128)} %norm_gain.1, bf16[1,4096,512]{2,1,0:T(8,128)(2,1)} %w_z.1, bf16[1,4096,512]{2,1,0:T(8,128)(2,1)} %w_x.1, bf16[1,4096,256]{2,1,0:T(8,128)(2,1)} %w_bc.1, bf16[1,8,4096]{2,1,0:T(8,128)(2,1)} %bitcast.1, ...), custom_call_target="tpu_custom_call" | custom-call | tf_op jit(solution)/shard_map/pallas_call | solution.py:411
  198.5 1.6 reshape.3

commit v3 on v2

v3 whole, which is shorter than its diff:
```python
import jax
import jax.numpy as jnp
from jax import lax
from jax.experimental import pallas as pl
from jax.experimental.pallas import tpu as pltpu
from jax.sharding import PartitionSpec as P

MESH = pl.DeviceIdType.MESH
F32 = jnp.float32
BF16 = jnp.bfloat16
EPS = 1e-05

SECTIONS = 8
MEMBERS = 16
SLICES = 4
SLICE = 64
UNIT = 16
UNITS = SLICES * SLICE // UNIT
RUNS = ((2, 8),)
WIDTH = 4096
OWN = WIDTH // MEMBERS
STATE = 128
CONV = 4
HEADS = 8
HEAD_DIM = 64
INNER = HEADS * HEAD_DIM
CHANNELS = 1024
BD = 2 * STATE + 128
GROUPS_IN = 4


def ring_distance(step):
    return min(step, 4 - step)


OFFSETS = sorted(
    [(dx, dy) for dx in range(4) for dy in range(4)],
    key=lambda o: -(ring_distance(o[0]) + ring_distance(o[1])),
)


def terms_of(value, count):
    terms = []
    for _ in range(count):
        terms.append(value.astype(BF16).astype(F32))
        value = value - terms[-1]
    return terms


def spread_over(value, places, count):
    parts = [jnp.dot(t.astype(BF16), places, preferred_element_type=F32) for t in terms_of(value, count)]
    return sum(parts[1:], parts[0])


def silu(v):
    return v / (1.0 + jnp.exp(-v))


def kernel(
    order,
    tokens,
    norm_gain,
    w_z,
    w_x,
    w_bc,
    w_dt,
    conv_x,
    conv_bc,
    dt_bias,
    decay_rate,
    skip_gain,
    inner_gain,
    w_out,
    out,
    tokens_v,
    gain_v,
    wz,
    wx,
    wbd,
    wdt,
    wout,
    cx,
    cbc,
    bias_v,
    rate_v,
    skip_v,
    inner_v,
    lhs_refs,
    sums_out_refs,
    sums_in_refs,
    squares_out,
    squares_in,
    fresh,
    rows_out,
    x_hist,
    bc_hist,
    state,
    small_sem,
    weight_sem,
    out_sem,
    lhs_sends,
    lhs_recvs,
    sums_sends,
    sums_recvs,
    squares_send,
    squares_recv,
    rows_send,
    rows_recv,
):
    section = lax.axis_index("pipe")
    dp = lax.axis_index("dp")
    tensor = lax.axis_index("tensor")
    me = dp * 2 + tensor
    my_x = tensor * 2 + lax.div(dp, 4)
    my_y = lax.rem(dp, 4)
    first = section == 0
    last = section == SECTIONS - 1

    def member(dx, dy):
        x, y = lax.rem(my_x + dx, 4), lax.rem(my_y + dy, 4)
        return (lax.rem(x, 2) * 4 + y) * 2 + lax.div(x, 2)

    def device(sec, m):
        return {"pipe": sec, "dp": lax.div(m, 2), "tensor": lax.rem(m, 2)}

    targets = [member(dx, dy) for dx, dy in OFFSETS]
    sources = [member(4 - dx, 4 - dy) for dx, dy in OFFSETS]

    def remote(src, dst, send, recv, sec, m):
        return pltpu.make_async_remote_copy(
            src_ref=src, dst_ref=dst, send_sem=send, recv_sem=recv, device_id=device(sec, m), device_id_type=MESH
        )

    def wait_bytes(ref, sem):
        pltpu.make_async_copy(ref, ref, sem).wait()

    small = [
        (norm_gain, gain_v),
        (w_dt.at[0], wdt),
        (conv_x.at[0], cx),
        (conv_bc.at[0], cbc),
        (dt_bias, bias_v),
        (decay_rate, rate_v),
        (skip_gain, skip_v),
        (inner_gain, inner_v),
    ]
    small_copies = [pltpu.make_async_copy(a, b, small_sem.at[i]) for i, (a, b) in enumerate(small)]
    token_copy = pltpu.make_async_copy(tokens, tokens_v, small_sem.at[len(small)])
    for copy in small_copies:
        copy.start()

    def weight_copies(c):
        rows = pl.ds(pl.multiple_of(c * OWN, OWN), OWN)
        return [
            pltpu.make_async_copy(w_bc.at[0, rows], wbd.at[rows, 0 : 2 * STATE], weight_sem.at[c, 0]),
            pltpu.make_async_copy(w_x.at[0, rows], wx.at[rows], weight_sem.at[c, 1]),
            pltpu.make_async_copy(w_z.at[0, rows], wz.at[rows], weight_sem.at[c, 2]),
        ]

    def out_copy(c):
        cols = pl.ds(pl.multiple_of(c * OWN, OWN), OWN)
        return pltpu.make_async_copy(w_out.at[0, :, cols], wout.at[c], out_sem.at[c])

    def load(c, carry):
        for copy in weight_copies(c):
            copy.start()
        return carry

    def load_out(c, carry):
        out_copy(c).start()
        return carry

    @pl.when(first)
    def _():
        token_copy.start()

    lax.fori_loop(0, MEMBERS, load, 0)

    barrier = pltpu.get_barrier_semaphore()

    def greet(sec, members):
        for m in members:
            pl.semaphore_signal(barrier, inc=1, device_id=device(sec, m), device_id_type=MESH)

    greet(section, sources[:-1])

    @pl.when(section > 0)
    def _():
        greet(section - 1, sources)

    x_hist[0:8, :] = jnp.zeros((8, INNER), F32)
    bc_hist[0:8, :] = jnp.zeros((8, 2 * STATE), F32)
    state[...] = jnp.zeros((STATE, INNER), F32)
    for copy in small_copies:
        copy.wait()

    diagonal = lax.broadcasted_iota(jnp.int32, (OWN, OWN), 0) == lax.broadcasted_iota(jnp.int32, (OWN, OWN), 1)

    def fold(c, carry):
        rows = pl.ds(pl.multiple_of(c * OWN, OWN), OWN)
        along = gain_v[0:1, rows]
        down = jnp.sum(jnp.where(diagonal, along, 0.0), axis=1, keepdims=True)
        steps = jnp.concatenate([wdt[:, rows].astype(F32) * along, jnp.zeros((128 - HEADS, OWN), F32)], axis=0)
        wbd[rows, 2 * STATE : BD] = jnp.transpose(steps).astype(BF16)
        for copy in weight_copies(c):
            copy.wait()
        wbd[rows, 0 : 2 * STATE] = (wbd[rows, 0 : 2 * STATE].astype(F32) * down).astype(BF16)
        wx[rows, :] = (wx[rows, :].astype(F32) * down).astype(BF16)
        wz[rows, :] = (wz[rows, :].astype(F32) * down).astype(BF16)
        return carry

    lax.fori_loop(0, MEMBERS, fold, 0)
    lax.fori_loop(0, MEMBERS, load_out, 0)

    @pl.when(first)
    def _():
        token_copy.wait()

    pl.semaphore_wait(barrier, MEMBERS - 1 + jnp.where(last, 0, MEMBERS))

    def load_out_wait(c, carry):
        out_copy(c).wait()
        return carry

    spread = (
        lax.div(lax.broadcasted_iota(jnp.int32, (HEADS, INNER), 1), HEAD_DIM)
        == lax.broadcasted_iota(jnp.int32, (HEADS, INNER), 0)
    ).astype(BF16)
    skip_wide = spread_over(skip_v[...], spread, 3)

    def front(run, k, unit):
        units = RUNS[run][0]
        length = units * UNIT
        lhs, lhs_recv = lhs_refs[run], lhs_recvs[run]
        sums_out, sums_in = sums_out_refs[run], sums_in_refs[run]
        sums_send, sums_recv = sums_sends[run], sums_recvs[run]

        @pl.when(first)
        def _():
            for u in range(units):
                place = order[lax.div(unit + u, SLICE // UNIT)]
                rows = pl.ds(pl.multiple_of(lax.rem(unit + u, SLICE // UNIT) * UNIT, UNIT), UNIT)
                for c in range(MEMBERS):
                    lhs[k, c, u] = tokens_v[place, rows, c * OWN : (c + 1) * OWN]

        bd_sum = jnp.zeros((length, BD), F32)
        x_sum = jnp.zeros((length, INNER), F32)
        z_sum = jnp.zeros((length, INNER), F32)
        squares = jnp.zeros((length, OWN), F32)
        per_group = MEMBERS // GROUPS_IN
        for g in range(GROUPS_IN):

            @pl.when(section > 0)
            def _():
                wait_bytes(lhs.at[k, pl.ds(0, per_group)], lhs_recv.at[k, g])

            for i in range(g * per_group, (g + 1) * per_group):
                c = sources[i]
                rows = pl.ds(pl.multiple_of(c * OWN, OWN), OWN)
                block = lhs[k, c].reshape(length, OWN)
                bd_sum = bd_sum + jnp.dot(block, wbd[rows, :], preferred_element_type=F32)
                x_sum = x_sum + jnp.dot(block, wx[rows, :], preferred_element_type=F32)
                z_sum = z_sum + jnp.dot(block, wz[rows, :], preferred_element_type=F32)
                wide = block.astype(F32)
                squares = squares + wide * wide
        scale = lax.rsqrt(jnp.sum(squares, axis=1, keepdims=True) * (1.0 / WIDTH) + EPS)
        dt_raw = bd_sum[:, 2 * STATE : 2 * STATE + HEADS] * scale
        bc_hist[8 : length + 8, :] = bd_sum[:, 0 : 2 * STATE] * scale
        x_hist[8 : length + 8, :] = x_sum * scale

        bc_conv = cbc[0:1, :] * bc_hist[5 : length + 5, :]
        x_conv = cx[0:1, :] * x_hist[5 : length + 5, :]
        for j in range(1, CONV):
            bc_conv = bc_conv + cbc[j : j + 1, :] * bc_hist[5 + j : length + 5 + j, :]
            x_conv = x_conv + cx[j : j + 1, :] * x_hist[5 + j : length + 5 + j, :]
        bc_act = silu(bc_conv)
        x_act = silu(x_conv)
        b_part = bc_act[:, 0:STATE].astype(BF16)
        c_part = bc_act[:, STATE:].astype(BF16)

        spread_rows = (
            lax.div(lax.broadcasted_iota(jnp.int32, (HEADS, HEADS * length), 1), length)
            == lax.broadcasted_iota(jnp.int32, (HEADS, HEADS * length), 0)
        ).astype(BF16)
        raised = dt_raw + bias_v[...]
        steps = jnp.maximum(raised, 0.0) + jnp.log1p(jnp.exp(-jnp.abs(raised)))
        lower = (
            lax.broadcasted_iota(jnp.int32, (length, 3 * length), 0)
            >= lax.rem(lax.broadcasted_iota(jnp.int32, (length, 3 * length), 1), length)
        ).astype(BF16)
        falls = jnp.concatenate(terms_of(-steps * rate_v[...], 3), axis=0).astype(BF16)
        cumulated = jnp.dot(lower, falls, preferred_element_type=F32)
        ending = cumulated[length - 1 : length, :]
        cum_rows = spread_over(cumulated, spread_rows, 3)
        step_rows = spread_over(steps, spread_rows, 2)
        grown = spread_over(jnp.exp(cumulated), spread, 2)
        remains = spread_over(jnp.exp(ending - cumulated) * steps, spread, 2)
        t_wide = lax.broadcasted_iota(jnp.int32, (length, HEADS * length), 0)
        s_wide = lax.rem(lax.broadcasted_iota(jnp.int32, (length, HEADS * length), 1), length)
        on_diag = t_wide == s_wide
        cum_row = jnp.sum(jnp.where(on_diag, cum_rows, 0.0), axis=0, keepdims=True)
        step_row = jnp.sum(jnp.where(on_diag, step_rows, 0.0), axis=0, keepdims=True)
        decays = jnp.exp(jnp.where(t_wide >= s_wide, cum_rows - cum_row, -1e30)) * step_row

        scores = lax.dot_general(
            c_part, jnp.concatenate([b_part] * HEADS, axis=0), (((1,), (1,)), ((), ())), preferred_element_type=F32
        )
        weighted = (scores * decays).astype(BF16)
        low = lax.broadcasted_iota(jnp.int32, (length, 128), 1) < HEAD_DIM
        blocks = []
        for h in range(HEADS):
            pair = x_act[:, 128 * (h // 2) : 128 * (h // 2 + 1)]
            mine = jnp.where(low, pair, 0.0) if h % 2 == 0 else jnp.where(low, 0.0, pair)
            parts = [mine if j == h // 2 else jnp.zeros((length, 128), F32) for j in range(HEADS // 2)]
            blocks.append(jnp.concatenate(parts, axis=1))
        inside = jnp.dot(weighted, jnp.concatenate(blocks, axis=0).astype(BF16), preferred_element_type=F32)
        carried = jnp.dot(c_part, state[...].astype(BF16), preferred_element_type=F32)
        y = inside + grown * carried + skip_wide * x_act

        gated = y * silu(z_sum * scale)
        mixed = (gated * inner_v[...]).astype(BF16)

        total = jnp.sum(gated * gated, axis=1, keepdims=True)
        on_row = lax.broadcasted_iota(jnp.int32, (length, 128), 0) == lax.broadcasted_iota(
            jnp.int32, (length, 128), 1
        )
        squares_out[unit] = jnp.sum(jnp.where(on_row, total, 0.0), axis=0, keepdims=True)

        @pl.when(unit == 0)
        def _():
            lax.fori_loop(0, MEMBERS, load_out_wait, 0)

        for i in range(MEMBERS):
            there = squares_in.at[unit, me]
            if i < MEMBERS - 1:
                remote(
                    squares_out.at[unit], there, squares_send.at[unit], squares_recv.at[unit], section, targets[i]
                ).start()
            else:
                pltpu.make_async_copy(squares_out.at[unit], there, squares_recv.at[unit]).start()

        for i in range(MEMBERS):
            m = targets[i]
            part = jnp.dot(mixed, wout[m], preferred_element_type=F32).astype(BF16)
            sums_out[k, m] = part.reshape(units, UNIT, OWN)
            if i < MEMBERS - 1:
                remote(
                    sums_out.at[k, m], sums_in.at[k, me], sums_send.at[k], sums_recv.at[k], section, m
                ).start()
            else:
                pltpu.make_async_copy(sums_out.at[k, m], sums_in.at[k, me], sums_recv.at[k]).start()
        state[...] = grown[length - 1 : length, :] * state[...] + lax.dot_general(
            b_part, (x_act * remains).astype(BF16), (((0,), (0,)), ((), ())), preferred_element_type=F32
        )
        x_hist[0:8, :] = x_hist[length : length + 8, :]
        bc_hist[0:8, :] = bc_hist[length : length + 8, :]

    def back(run, k, unit):
        units, pieces = RUNS[run]
        lhs, sums_in = lhs_refs[run], sums_in_refs[run]
        length = units * UNIT
        wait_bytes(squares_in.at[unit], squares_recv.at[unit])
        on_row = lax.broadcasted_iota(jnp.int32, (length, 128), 0) == lax.broadcasted_iota(
            jnp.int32, (length, 128), 1
        )
        factors = []
        for g in range(MEMBERS // 2):
            total = squares_in[unit, 2 * g] + squares_in[unit, 2 * g + 1]
            along = lax.rsqrt(total * (1.0 / CHANNELS) + EPS)
            factors.append(jnp.sum(jnp.where(on_row, along, 0.0), axis=1, keepdims=True))
        wait_bytes(sums_in.at[k], sums_recvs[run].at[k])
        total = lhs[k, me].reshape(length, OWN).astype(F32)
        for g in range(MEMBERS // 2):
            both = sums_in[k, 2 * g].astype(F32) + sums_in[k, 2 * g + 1].astype(F32)
            total = total + both.reshape(length, OWN) * factors[g]
        updated = total.astype(BF16).reshape(units, UNIT, OWN)
        for u in range(units):
            fresh[unit + u] = updated[u]

        @pl.when(section < SECTIONS - 1)
        def _():
            for i in range(MEMBERS):
                remote(
                    fresh.at[pl.ds(unit, units)],
                    lhs.at[k, me],
                    lhs_sends[run].at[k],
                    lhs_recvs[run].at[k, i // (MEMBERS // GROUPS_IN)],
                    section + 1,
                    targets[i],
                ).start()

    def give_rows(quads):
        for q in quads:
            quad = jnp.concatenate([fresh[4 * s + q] for s in range(SLICES)], axis=0)
            for i in range(4):
                to = lax.broadcasted_iota(jnp.int32, (16, 64), 0)
                of = lax.broadcasted_iota(jnp.int32, (16, 64), 1)
                pick = (of == lax.div(to, 4) * 16 + lax.rem(to, 4) + 4 * i).astype(BF16)
                rows_out[4 * q + i] = jnp.dot(pick, quad, preferred_element_type=F32).astype(BF16)
        for q in quads:
            for i in range(4):
                m = 4 * q + i

                @pl.when(m != me)
                def _():
                    remote(rows_out.at[m], mine, rows_send.at[0], rows_recv.at[0], section, m).start()

                @pl.when(m == me)
                def _():
                    pltpu.make_async_copy(rows_out.at[m], mine, rows_recv.at[0]).start()

    mine = out.at[:, pl.ds(pl.multiple_of(me * OWN, OWN), OWN)]
    early = range(4 - RUNS[-1][0])

    base = 0
    for run, (units, pieces) in enumerate(RUNS):

        def step(k, carry, run=run, units=units, pieces=pieces, base=base):
            unit = base + k * units

            if run == len(RUNS) - 1 and early:

                @pl.when(k == pieces - 1)
                def _():
                    give_rows(early)

            front(run, k, unit)
            back(run, k, unit)
            return carry

        lax.fori_loop(0, pieces, step, 0)
        base += units * pieces

    give_rows(range(len(early), 4))

    base = 0
    for run, (units, pieces) in enumerate(RUNS):

        def drain(k, carry, run=run, units=units, base=base):
            unit = base + k * units
            wait_bytes(squares_in.at[unit, pl.ds(0, MEMBERS - 1)], squares_send.at[unit])
            wait_bytes(sums_in_refs[run].at[k, pl.ds(0, MEMBERS - 1)], sums_sends[run].at[k])

            @pl.when(section < SECTIONS - 1)
            def _():
                wait_bytes(lhs_refs[run].at[k], lhs_sends[run].at[k])

            return carry

        lax.fori_loop(0, pieces, drain, 0)
        base += units * pieces
    wait_bytes(rows_out.at[pl.ds(0, MEMBERS - 1)], rows_send.at[0])
    wait_bytes(rows_out, rows_recv.at[0])


def local(tokens, slice_order, norm_gain, w_z, w_x, w_bc, w_dt, *rest):
    hbm = pl.BlockSpec(memory_space=pltpu.HBM)
    dma = pltpu.SemaphoreType.DMA
    args = (tokens, norm_gain, w_z, w_x, w_bc, jnp.swapaxes(w_dt, 1, 2), *rest)
    rows = pl.pallas_call(
        kernel,
        out_shape=jax.ShapeDtypeStruct((SLICES * SLICE // MEMBERS, WIDTH), BF16),
        in_specs=[pl.BlockSpec(memory_space=pltpu.SMEM)] + [hbm] * len(args),
        out_specs=pl.BlockSpec(memory_space=pltpu.VMEM),
        scratch_shapes=[
            pltpu.VMEM((SLICES, SLICE, WIDTH), BF16),
            pltpu.VMEM((1, WIDTH), F32),
            pltpu.VMEM((WIDTH, INNER), BF16),
            pltpu.VMEM((WIDTH, INNER), BF16),
            pltpu.VMEM((WIDTH, BD), BF16),
            pltpu.VMEM((HEADS, WIDTH), BF16),
            pltpu.VMEM((MEMBERS, INNER, OWN), BF16),
            pltpu.VMEM((CONV, INNER), F32),
            pltpu.VMEM((CONV, 2 * STATE), F32),
            pltpu.VMEM((1, HEADS), F32),
            pltpu.VMEM((1, HEADS), F32),
            pltpu.VMEM((1, HEADS), F32),
            pltpu.VMEM((1, INNER), F32),
            [pltpu.VMEM((pieces, MEMBERS, units, UNIT, OWN), BF16) for units, pieces in RUNS],
            [pltpu.VMEM((pieces, MEMBERS, units, UNIT, OWN), BF16) for units, pieces in RUNS],
            [pltpu.VMEM((pieces, MEMBERS, units, UNIT, OWN), BF16) for units, pieces in RUNS],
            pltpu.VMEM((UNITS, 1, 128), F32),
            pltpu.VMEM((UNITS, MEMBERS, 1, 128), F32),
            pltpu.VMEM((UNITS, UNIT, OWN), BF16),
            pltpu.VMEM((MEMBERS, 16, OWN), BF16),
            pltpu.VMEM((SLICE + 8, INNER), F32),
            pltpu.VMEM((SLICE + 8, 2 * STATE), F32),
            pltpu.VMEM((STATE, INNER), F32),
            dma((9,)),
            dma((MEMBERS, 3)),
            dma((MEMBERS,)),
            [dma((pieces,)) for _, pieces in RUNS],
            [dma((pieces, GROUPS_IN)) for _, pieces in RUNS],
            [dma((pieces,)) for _, pieces in RUNS],
            [dma((pieces,)) for _, pieces in RUNS],
            dma((UNITS,)),
            dma((UNITS,)),
            dma((1,)),
            dma((1,)),
        ],
        compiler_params=pltpu.CompilerParams(
            collective_id=0, has_side_effects=True, vmem_limit_bytes=60 * 1024 * 1024
        ),
    )(slice_order, *args)
    return rows.reshape(1, SLICES, SLICE // MEMBERS, WIDTH)


def solution(mesh):
    both = ("dp", "tensor")
    placed = (
        P(),
        P(),
        P("pipe", None),
        P("pipe", None, both),
        P("pipe", None, both),
        P("pipe", None, "dp"),
        P("pipe", None, both),
        P("pipe", None, both),
        P("pipe", None, "dp"),
        P("pipe", both),
        P("pipe", both),
        P("pipe", both),
        P("pipe", both),
        P("pipe", both, None),
    )
    return jax.shard_map(
        local,
        mesh=mesh,
        in_specs=placed,
        out_specs=P("pipe", None, both, None),
        check_vma=False,
    )
```

time: 201 us -> 185 us (0.920)
  Pallas kernels: 198 us -> 183 us
    pallas_call x1, Pallas kernels: 198 us -> 183 us  [local(): pl.pallas_call(kernel, out_shape=jax.ShapeDtypeStruct((SLICES * SLICE //...]
where the time goes in v3:
time: 185 us
  Pallas kernels  183 us (99%)
    pallas_call x1, Pallas kernels, local(): pl.pallas_call(kernel, out_shape=jax.ShapeDtypeStruct((SLICES * SLICE //...  183 us

profile of v3, /device:TPU:99, one launch (start us, length us, event | category | flops | bytes accessed | tf_op | source)
XLA Modules:
  0.0 184.8 jit_solution(4791446838240964079)
XLA Ops:
  0.0 183.2 %shard_map.136 = bf16[16,4096]{1,0:T(8,128)(2,1)} custom-call(s32[4]{0:T(128)} %order.1, bf16[4,64,4096]{2,1,0:T(8,128)(2,1)} %tokens.1, f32[1,4096]{1,0:T(1,128)} %norm_gain.1, bf16[1,4096,512]{2,1,0:T(8,128)(2,1)} %w_z.1, bf16[1,4096,512]{2,1,0:T(8,128)(2,1)} %w_x.1, bf16[1,4096,256]{2,1,0:T(8,128)(2,1)} %w_bc.1, bf16[1,8,4096]{2,1,0:T(8,128)(2,1)} %bitcast.1, ...), custom_call_target="tpu_custom_call" | custom-call | tf_op jit(solution)/shard_map/pallas_call | solution.py:460
  183.2 1.6 reshape.3

commit v4 on v3

--- a/solution.py
+++ b/solution.py
@@ -200,7 +200,7 @@
         rows = pl.ds(pl.multiple_of(c * OWN, OWN), OWN)
         along = gain_v[0:1, rows]
         down = jnp.sum(jnp.where(diagonal, along, 0.0), axis=1, keepdims=True)
-        steps = jnp.concatenate([wdt[:, rows].astype(F32) * along, jnp.zeros((128 - HEADS, OWN), F32)], axis=0)
+        steps = jnp.concatenate([wdt[:, rows].astype(F32) * along, jnp.zeros((128 - UNIT, OWN), F32)], axis=0)
         wbd[rows, 2 * STATE : BD] = jnp.transpose(steps).astype(BF16)
         for copy in weight_copies(c):
             copy.wait()
@@ -456,7 +456,8 @@
 def local(tokens, slice_order, norm_gain, w_z, w_x, w_bc, w_dt, *rest):
     hbm = pl.BlockSpec(memory_space=pltpu.HBM)
     dma = pltpu.SemaphoreType.DMA
-    args = (tokens, norm_gain, w_z, w_x, w_bc, jnp.swapaxes(w_dt, 1, 2), *rest)
+    steps = jnp.pad(jnp.swapaxes(w_dt, 1, 2), ((0, 0), (0, UNIT - HEADS), (0, 0)))
+    args = (tokens, norm_gain, w_z, w_x, w_bc, steps, *rest)
     rows = pl.pallas_call(
         kernel,
         out_shape=jax.ShapeDtypeStruct((SLICES * SLICE // MEMBERS, WIDTH), BF16),
@@ -468,7 +469,7 @@
             pltpu.VMEM((WIDTH, INNER), BF16),
             pltpu.VMEM((WIDTH, INNER), BF16),
             pltpu.VMEM((WIDTH, BD), BF16),
-            pltpu.VMEM((HEADS, WIDTH), BF16),
+            pltpu.VMEM((UNIT, WIDTH), BF16),
             pltpu.VMEM((MEMBERS, INNER, OWN), BF16),
             pltpu.VMEM((CONV, INNER), F32),
             pltpu.VMEM((CONV, 2 * STATE), F32),

time: 185 us -> 187 us (1.011)
  no operation moved by 1% of the time
where the time goes in v4:
time: 187 us; the launch traced here: 186 us
  Pallas kernels  183 us (98%)
  local copies, waits for them, and re-layouts  3.12 us (2%)
    pallas_call x1, Pallas kernels, local(): pl.pallas_call(kernel, out_shape=jax.ShapeDtypeStruct((SLICES * SLICE //...  183 us

profile of v4, /device:TPU:99, one launch (start us, length us, event | category | flops | bytes accessed | tf_op | source)
XLA Modules:
  0.0 186.4 jit_solution(5630977254468427967)
XLA Ops:
  0.0 1.5 pad.4.w_dt
  1.5 183.2 %shard_map.136 = bf16[16,4096]{1,0:T(8,128)(2,1)} custom-call(s32[4]{0:T(128)} %order.1, bf16[4,64,4096]{2,1,0:T(8,128)(2,1)} %tokens.1, f32[1,4096]{1,0:T(1,128)} %norm_gain.1, bf16[1,4096,512]{2,1,0:T(8,128)(2,1)} %w_z.1, bf16[1,4096,512]{2,1,0:T(8,128)(2,1)} %w_x.1, bf16[1,4096,256]{2,1,0:T(8,128)(2,1)} %w_bc.1, bf16[1,16,4096]{2,1,0:T(8,128)(2,1)} %pad.4.w_dt, ...), custom_call_target="tpu_custom_call" | custom-call | tf_op jit(solution)/shard_map/pallas_call | solution.py:461
  184.8 1.6 reshape.3

commit v5 on v3

--- a/solution.py
+++ b/solution.py
@@ -77,7 +77,6 @@
     wz,
     wx,
     wbd,
-    wdt,
     wout,
     cx,
     cbc,
@@ -136,7 +135,6 @@
 
     small = [
         (norm_gain, gain_v),
-        (w_dt.at[0], wdt),
         (conv_x.at[0], cx),
         (conv_bc.at[0], cbc),
         (dt_bias, bias_v),
@@ -200,7 +198,7 @@
         rows = pl.ds(pl.multiple_of(c * OWN, OWN), OWN)
         along = gain_v[0:1, rows]
         down = jnp.sum(jnp.where(diagonal, along, 0.0), axis=1, keepdims=True)
-        steps = jnp.concatenate([wdt[:, rows].astype(F32) * along, jnp.zeros((128 - HEADS, OWN), F32)], axis=0)
+        steps = jnp.concatenate([w_dt[0, :, rows].astype(F32) * along, jnp.zeros((128 - HEADS, OWN), F32)], axis=0)
         wbd[rows, 2 * STATE : BD] = jnp.transpose(steps).astype(BF16)
         for copy in weight_copies(c):
             copy.wait()
@@ -460,7 +458,8 @@
     rows = pl.pallas_call(
         kernel,
         out_shape=jax.ShapeDtypeStruct((SLICES * SLICE // MEMBERS, WIDTH), BF16),
-        in_specs=[pl.BlockSpec(memory_space=pltpu.SMEM)] + [hbm] * len(args),
+        in_specs=[pl.BlockSpec(memory_space=pltpu.SMEM)]
+        + [pl.BlockSpec(memory_space=pltpu.VMEM) if i == 5 else hbm for i in range(len(args))],
         out_specs=pl.BlockSpec(memory_space=pltpu.VMEM),
         scratch_shapes=[
             pltpu.VMEM((SLICES, SLICE, WIDTH), BF16),
@@ -468,7 +467,6 @@
             pltpu.VMEM((WIDTH, INNER), BF16),
             pltpu.VMEM((WIDTH, INNER), BF16),
             pltpu.VMEM((WIDTH, BD), BF16),
-            pltpu.VMEM((HEADS, WIDTH), BF16),
             pltpu.VMEM((MEMBERS, INNER, OWN), BF16),
             pltpu.VMEM((CONV, INNER), F32),
             pltpu.VMEM((CONV, 2 * STATE), F32),

time: 185 us -> 185 us (level)
  no operation moved by 1% of the time
where the time goes in v5:
time: 185 us
  Pallas kernels  183 us (99%)
    pallas_call x1, Pallas kernels, local(): pl.pallas_call(kernel, out_shape=jax.ShapeDtypeStruct((SLICES * SLICE //...  183 us

profile of v5, /device:TPU:99, one launch (start us, length us, event | category | flops | bytes accessed | tf_op | source)
XLA Modules:
  0.0 185.0 jit_solution(4893591912908061182)
XLA Ops:
  0.0 183.3 %shard_map.136 = bf16[16,4096]{1,0:T(8,128)(2,1)} custom-call(s32[4]{0:T(128)} %order.1, bf16[4,64,4096]{2,1,0:T(8,128)(2,1)} %tokens.1, f32[1,4096]{1,0:T(1,128)} %norm_gain.1, bf16[1,4096,512]{2,1,0:T(8,128)(2,1)} %w_z.1, bf16[1,4096,512]{2,1,0:T(8,128)(2,1)} %w_x.1, bf16[1,4096,256]{2,1,0:T(8,128)(2,1)} %w_bc.1, bf16[1,8,4096]{2,1,0:T(8,128)(2,1)} %bitcast.1, ...), custom_call_target="tpu_custom_call" | custom-call | tf_op jit(solution)/shard_map/pallas_call | solution.py:458
  183.4 1.6 reshape.3
